TPU v7x, 256 devices: a whole 4x4x8 slice. The times are simulated.
256 devices in a mesh: section: 16 (over z_lo, y, core), enc: 16 (over z_hi, x).
Axes of the slice: x: 4, y: 4, z: 8 (z_hi: 4, z_lo: 2; z = z_hi * 2 + z_lo), core: 2. Of those that a mesh axis runs over, the one named last changes fastest.
Arguments:
- latents: bfloat16 [48, 64, 1280], P('enc', 'section'), may hold values from -4 to 4
- key_weight: bfloat16 [16, 1280, 4096], P('section', None, 'enc'), may hold values from -0.1118034 to 0.1118034
- value_weight: bfloat16 [16, 1280, 4096], P('section', None, 'enc'), may hold values from -0.15625 to 0.15625
- gate_logit: float32 [16], P('section'), may hold values from 0.3 to 1.5
- queries: bfloat16 [16, 1024, 4096], P('section', None, 'enc'), may hold values from -150 to 150
- cotangent: bfloat16 [16, 1024, 4096], P('section', None, 'enc'), may hold values from -6 to 6
- image_counts: int32 [16], replicated, may hold values from 1 to 3, as said below
- token_image: int32 [1024], replicated, may hold values from 0 to 31, as said below
Outputs:
- attended: bfloat16 [16, 1024, 4096], P('section', None, 'enc')
- grad_queries: bfloat16 [16, 1024, 4096], P('section', None, 'enc')
- grad_latents: float32 [48, 64, 1280], P('enc', 'section')
Inputs may be any that keep to these rules, and one draw needn't show every extreme that they name: `image_counts`: the images of all owners sum to 32. `token_image`: never falls along the tokens; every image has at least 8 tokens, and some image exactly that many.
All inputs are finite; a program needn't handle non-finite values.
Results may differ from a plain program's by a relative error of at most 0.028.
Values may be sent and summed in bfloat16 or wider, within the bound.
A program may use at most 128 MiB of HBM per device.

v0:
```python
import math

import jax
import jax.numpy as jnp
from jax import lax
from jax.sharding import PartitionSpec as P

HD = 128
IMG_DEV = 2
TXT_IMG = 32


def image_slots(image_counts, images, capacity):
    owners = image_counts.shape[0]
    image_ends = jnp.cumsum(image_counts)
    image_starts = image_ends - image_counts
    image_index = jnp.arange(images, dtype=jnp.int32)
    owner_of = jnp.sum((image_index[:, None] >= image_ends[None, :]).astype(jnp.int32), axis=1)
    owner_match = owner_of[:, None] == jnp.arange(owners, dtype=jnp.int32)[None, :]
    first_image = jnp.sum(jnp.where(owner_match, image_starts[None, :], 0), axis=1)
    return owner_of * capacity + image_index - first_image


def slot_images(image_counts, capacity):
    image_ends = jnp.cumsum(image_counts)
    image_starts = image_ends - image_counts
    slot_index = jnp.arange(image_counts.shape[0] * capacity, dtype=jnp.int32)
    slot_place = slot_index % capacity
    counts_of = jnp.repeat(image_counts, capacity)
    starts_of = jnp.repeat(image_starts, capacity)
    occupied = slot_place < counts_of
    return (occupied, jnp.where(occupied, starts_of + slot_place, 0))


def on_device(
    latents, key_weight, value_weight, gate_logit, queries, cotangent, image_counts, token_image
):
    f32 = jnp.float32
    capacity = latents.shape[0]
    owners = image_counts.shape[0]
    images = IMG_DEV * owners
    latent_width = latents.shape[2]
    head_width = key_weight.shape[2]
    heads_here = head_width // HD
    weights = jnp.concatenate([key_weight[0], value_weight[0]], axis=1)
    image_slot = image_slots(image_counts, images, capacity)
    gathered = lax.all_gather(latents, "section", axis=1, tiled=True)
    latent_count = gathered.shape[1]
    shard_piece = lax.all_gather(gathered, "enc", axis=0, tiled=True)
    flattened = shard_piece.reshape(-1, latent_width)
    result = jnp.dot(flattened, weights, preferred_element_type=f32).astype(jnp.bfloat16)
    projected = result.reshape(shard_piece.shape[0], latent_count, 2 * head_width)
    projected = jnp.take(projected, image_slot, axis=0)
    key_rows = projected[:, :, :head_width].reshape(images * latent_count, heads_here, HD)
    value_rows = projected[:, :, head_width:].reshape(images * latent_count, heads_here, HD)
    score_scale = 1.0 / math.sqrt(HD)
    factor = jnp.tanh(gate_logit[0])
    tokens = queries.shape[1]
    block_rows = math.gcd(tokens, 128)
    block_count = tokens // block_rows
    shortest = TXT_IMG - 3 * TXT_IMG // 4
    band = min(images, block_rows // shortest + 2)
    band_rows = band * latent_count
    band_image = jnp.arange(band_rows, dtype=jnp.int32) // latent_count

    def one_block(carry, block_inputs):
        grad_keys, grad_values = carry
        query_block, cot_block, image_block = block_inputs
        start = jnp.clip(image_block[0], 0, images - band)
        first_row = start * latent_count
        key_band = lax.dynamic_slice_in_dim(key_rows, first_row, band_rows, 0)
        value_band = lax.dynamic_slice_in_dim(value_rows, first_row, band_rows, 0)
        column_image = start + band_image
        scores = (
            jnp.einsum("thd,shd->hts", query_block, key_band, preferred_element_type=f32)
            * score_scale
        )
        same_image = (image_block[:, None] == column_image[None, :])[None]
        scores = jnp.where(same_image, scores, -jnp.inf)
        row_max = jnp.max(scores, axis=2, keepdims=True)
        exponent = jnp.exp(scores - row_max)
        probs = exponent / jnp.sum(exponent, axis=2, keepdims=True)
        probs_b = probs.astype(jnp.bfloat16)
        mixture = jnp.einsum("hts,shd->thd", probs_b, value_band, preferred_element_type=f32)
        attended = (factor * mixture).astype(jnp.bfloat16)
        grad_mix = (factor * cot_block.astype(f32)).astype(jnp.bfloat16)
        grad_probs = jnp.einsum("thd,shd->hts", grad_mix, value_band, preferred_element_type=f32)
        weighted = jnp.sum(probs * grad_probs, axis=2, keepdims=True)
        grad_scores = (probs * (grad_probs - weighted) * score_scale).astype(jnp.bfloat16)
        grad_query = jnp.einsum(
            "hts,shd->thd", grad_scores, key_band, preferred_element_type=f32
        ).astype(jnp.bfloat16)
        key_part = lax.dynamic_slice_in_dim(grad_keys, first_row, band_rows, 0)
        key_part = key_part + jnp.einsum(
            "hts,thd->shd", grad_scores, query_block, preferred_element_type=f32
        )
        value_part = lax.dynamic_slice_in_dim(grad_values, first_row, band_rows, 0)
        value_part = value_part + jnp.einsum(
            "hts,thd->shd", probs_b, grad_mix, preferred_element_type=f32
        )
        grad_keys = lax.dynamic_update_slice_in_dim(grad_keys, key_part, first_row, 0)
        grad_values = lax.dynamic_update_slice_in_dim(grad_values, value_part, first_row, 0)
        return ((grad_keys, grad_values), (attended, grad_query))

    zeros = jnp.zeros((images * latent_count, heads_here, HD), f32)
    block_inputs = (
        queries[0].reshape(block_count, block_rows, heads_here, HD),
        cotangent[0].reshape(block_count, block_rows, heads_here, HD),
        token_image.reshape(block_count, block_rows),
    )
    (grad_keys, grad_values), (attended, grad_query) = lax.scan(
        one_block, (zeros, zeros), block_inputs
    )
    attended = attended.reshape(1, tokens, head_width)
    grad_queries = grad_query.reshape(1, tokens, head_width)
    grad_both = jnp.concatenate(
        [
            grad_keys.reshape(images, latent_count, head_width),
            grad_values.reshape(images, latent_count, head_width),
        ],
        axis=2,
    ).astype(jnp.bfloat16)
    occupied, source_image = slot_images(image_counts, capacity)
    in_slots = jnp.where(
        occupied[:, None, None],
        jnp.take(grad_both, source_image, axis=0),
        jnp.zeros((), jnp.bfloat16),
    )
    reduced = lax.psum_scatter(
        lax.dot_general(
            in_slots, weights, (((in_slots.ndim - 1,), (1,)), ((), ())), preferred_element_type=f32
        ).astype(jnp.bfloat16),
        "enc",
        scatter_dimension=0,
        tiled=True,
    )
    grad_latents = lax.psum_scatter(reduced, "section", scatter_dimension=1, tiled=True).astype(
        jnp.float32
    )
    return (attended, grad_queries, grad_latents)


def solution(mesh):
    placed = (
        P("enc", "section", None),
        P("section", None, "enc"),
        P("section", None, "enc"),
        P("section"),
        P("section", None, "enc"),
        P("section", None, "enc"),
        P(),
        P(),
    )
    return jax.shard_map(
        on_device,
        mesh=mesh,
        in_specs=placed,
        out_specs=(P("section", None, "enc"), P("section", None, "enc"), P("enc", "section", None)),
        check_vma=False,
    )
```

profile of v0, /device:TPU:8, one launch (start us, length us, event | category | flops | bytes accessed | tf_op | source)
XLA Modules:
  0.0 683.6 jit_solution(17566225580464475887)
XLA Ops:
  8.1 19.9 %all_gather.6 = bf16[3,64,1280]{2,0,1:T(4,128)(2,1)S(1)} all-gather(bf16[3,4,1280]{2,0,1:T(4,128)(2,1)S(1)} %copy.58), channel_id=1, replica_groups=mesh['section'=16,'enc'=16] {'section'}, dimensions={1}, use_global_device_ids=true | all-gather | bytes 522240 | tf_op jit(solution)/shard_map/all_gather | solution.py:47
  32.5 99.3 %all-gather.2.cloned.1.call-done = bf16[48,64,1280]{2,1,0:T(8,128)(2,1)} async-done(((bf16[3,64,1280]{2,1,0:T(8,128)(2,1)}), bf16[48,64,1280]{2,1,0:T(8,128)(2,1)}) %all-gather.2.cloned.1.call-update) | async-done | bytes 7864336 | tf_op jit(solution)/shard_map/all_gather | solution.py:49
  131.8 9.0 %fusion.48 = bf16[3072,512]{0,1:T(8,128)(2,1)} fusion(bf16[3072,1280]{1,0:T(8,128)(2,1)} %bitcast.86, bf16[1280,256]{1,0:T(8,128)(2,1)S(1)} %bitcast.87, bf16[1280,256]{1,0:T(8,128)(2,1)S(1)} %bitcast.89), kind=kOutput, calls=%fused_computation.62 | convolution fusion | flops 4030726144 | bytes 12320768 | tf_op jit(solution)/shard_map/dot_general | solution.py:51
  152.7 255.6 %while.17 = (s32[]{:T(128)}, f32[2048,2,128]{0,2,1:T(8,128)}, f32[2048,2,128]{0,2,1:T(8,128)}, bf16[8,128,2,128]{3,2,1,0:T(2,128)(2,1)}, bf16[8,128,2,128]{3,2,1...) while((s32[]{:T(128)}, f32[2048,2,128]{0,2,1:T(8,128)}, ...), condition=%wide.region_7.8_spmd.clone, body=%wide.region_3.7_spmd.clone.sunk | while | flops 460519424 | bytes 27707204 | solution.py:111
  173.6 5.8 dynamic_update_slice.24
  179.4 5.8 dynamic_update_slice.23
  206.1 6.3 dynamic_update_slice.24
  212.3 6.3 dynamic_update_slice.23
  239.5 6.2 dynamic_update_slice.24
  245.7 6.3 dynamic_update_slice.23
  265.0 3.9 fusion.101
  272.9 5.5 dynamic_update_slice.24
  278.4 5.5 dynamic_update_slice.23
  304.6 5.1 dynamic_update_slice.24
  309.8 5.2 dynamic_update_slice.23
  335.8 5.1 dynamic_update_slice.24
  340.9 5.2 dynamic_update_slice.23
  366.9 5.1 dynamic_update_slice.24
  372.0 5.2 dynamic_update_slice.23
  398.0 5.1 dynamic_update_slice.24
  403.2 5.2 dynamic_update_slice.23
  419.4 9.2 %convolution_convert_fusion.1 = bf16[48,64,1280]{2,1,0:T(8,128)(2,1)} fusion(bf16[48,64,512]{2,1,0:T(8,128)(2,1)} %gather_fusion.1, pred[48]{0:T(512)(128)(4,1)S(1)} %get-tuple-element.158, pred[48]{0:T(512)(128)(4,1)S(1)} %get-tuple-element.157, bf16[1280,256]{1,0:T(8,128)(2,1)S(1)} %bitcast.88, bf16[1280,256]{1,0:T(8,128)(2,1)S(1)} %bitcast.90), kind=kOutput, calls=%fused_computation.60 | convolution fusion | flops 4036231168 | bytes 12320864 | tf_op jit(solution)/shard_map/dot_general | solution.py:130
  428.7 127.0 %reduce-scatter.3.cloned.1.call-done = bf16[3,64,1280]{2,1,0:T(8,128)(2,1)} async-done(((bf16[48,64,1280]{2,1,0:T(8,128)(2,1)}), bf16[3,64,1280]{2,1,0:T(8,128)(2,1)}) %reduce-scatter.3.cloned.1.call-update) | async-done | bytes 491536 | tf_op jit(solution)/shard_map/reduce_scatter | solution.py:129
  559.2 116.5 %all-reduce.3.cloned.1.call-done = bf16[3,64,1280]{2,1,0:T(8,128)(2,1)} async-done(((bf16[3,64,1280]{2,1,0:T(8,128)(2,1)}), bf16[3,64,1280]{2,1,0:T(8,128)(2,1)}) %all-reduce.3.cloned.1.call-update) | async-done | bytes 491536
  (225 shorter events, 193.5 us)
Async XLA Ops:
  7.2 21.7 %copy-start.7 = (s32[16]{0:T(128)S(1)}, s32[16]{0:T(128)}, u32[]{:S(2)}) copy-start(s32[16]{0:T(128)} %param.16) | copy-start | bytes 196
  7.2 23.2 %copy-start.3 = (bf16[1,1024,256]{2,1,0:T(8,128)(2,1)S(1)}, bf16[1,1024,256]{2,1,0:T(8,128)(2,1)}, u32[]{:S(2)}) copy-start(bf16[1,1024,256]{2,1,0:T(8,128)(2,1)} %param.14) | copy-start | bytes 1572868
  7.2 124.6 %all-gather.2.cloned.1.call-start = ((), (), s32[]{:S(2)}) async-start(), calls=%async_computation.1 | async-start | bytes 8355840 | tf_op jit(solution)/shard_map/all_gather | solution.py:49
  28.0 3.3 copy-start.4
  28.8 103.0 %copy-start.8 = (bf16[1,1280,256]{2,1,0:T(8,128)(2,1)S(1)}, bf16[1,1280,256]{2,1,0:T(8,128)(2,1)}, u32[]{:S(2)}) copy-start(bf16[1,1280,256]{2,1,0:T(8,128)(2,1)} %param.12) | copy-start | bytes 1966084
  28.8 103.0 %copy-start.10 = (bf16[1,1280,256]{2,1,0:T(8,128)(2,1)S(1)}, bf16[1,1280,256]{2,1,0:T(8,128)(2,1)}, u32[]{:S(2)}) copy-start(bf16[1,1280,256]{2,1,0:T(8,128)(2,1)} %param.11) | copy-start | bytes 1966084
  28.8 526.8 %reduce-scatter.3.cloned.1.call-start = ((), (), s32[]{:S(2)}) async-start(), calls=%async_computation.2 | async-start | bytes 8355840 | tf_op jit(solution)/shard_map/reduce_scatter | solution.py:129
  156.0 3.7 copy-start.2
  188.4 3.7 copy-start.2
  221.9 3.7 copy-start.2
  255.2 3.7 copy-start.2
  287.1 3.7 copy-start.2
  318.2 3.7 copy-start.2
  349.3 3.7 copy-start.2
  380.5 3.7 copy-start.2
  410.9 2.0 copy-start
  413.8 1.5 copy-start.1
  416.7 2.6 copy-start.9
  416.8 2.6 copy-start.11
  428.6 127.1 %copy-start.12 = (u32[256]{0:T(256)S(1)}, u32[256]{0:T(256)}, u32[]{:S(2)}) copy-start(u32[256]{0:T(256)} %constant.106) | copy-start | bytes 3076
  428.6 128.3 %copy-start.5 = (bf16[8,128,2,128]{3,2,1,0:T(2,128)(2,1)S(1)}, bf16[8,128,2,128]{3,2,1,0:T(2,128)(2,1)}, u32[]{:S(2)}) copy-start(bf16[8,128,2,128]{3,2,1,0:T(2,128)(2,1)} %get-tuple-element.69) | copy-start | bytes 1572868
  428.6 129.4 %copy-start.6 = (bf16[8,128,2,128]{3,2,1,0:T(2,128)(2,1)S(1)}, bf16[8,128,2,128]{3,2,1,0:T(2,128)(2,1)}, u32[]{:S(2)}) copy-start(bf16[8,128,2,128]{3,2,1,0:T(2,128)(2,1)} %get-tuple-element.68) | copy-start | bytes 1572868
  428.6 247.0 %all-reduce.3.cloned.1.call-start = ((), (), s32[]{:S(2)}) async-start(), calls=%async_computation.3 | async-start | bytes 983040
Sparse Core Ops, SparseCore 0:
  28.9 102.8 all-gather.1
  428.7 126.8 reduce-scatter.2
  558.5 117.1 all-reduce.2
where the time goes:
time: 692 us; the launch traced here: 684 us
  waiting for transfers between devices  343 us (50%)
  local copies, waits for them, and re-layouts  169 us (24%)
  matrix products  128 us (18%)
  blocking collectives  19.9 us (3%)
  between operations  15.3 us (2%)
  other arithmetic  8.22 us (1%)
    reduce_scatter x1, waiting for transfers between devices, on_device(): lax.psum_scatter(lax.dot_general(in_slots, weights, (((in_slots.ndim - 1,...  127 us
    unnamed x4, waiting for transfers between devices  117 us
    all_gather x1, waiting for transfers between devices, on_device(): shard_piece = lax.all_gather(gathered, 'enc', axis=0, tiled=True)  99.3 us
    dynamic_update_slice x8, local copies, waits for them, and re-layouts, one_block(): lax.dynamic_update_slice_in_dim(grad_keys, key_part, first_row, 0)  44.6 us
    dynamic_update_slice x8, local copies, waits for them, and re-layouts, one_block(): lax.dynamic_update_slice_in_dim(grad_values, value_part, first_row, 0)  44.4 us
    dot_general x8, matrix products, one_block(): jnp.einsum('hts,shd->thd', grad_scores, key_band, preferred_element_type=...  31.4 us
    dot_general x8, matrix products, one_block(): jnp.einsum('hts,thd->shd', grad_scores, query_block, preferred_element_ty...  31.3 us
    all_gather x1, blocking collectives, on_device(): gathered = lax.all_gather(latents, 'section', axis=1, tiled=True)  19.9 us
  transfers between devices with their start and end apart: 3, of which 3 were waited for; matrix products, arithmetic and copies ran while one was open for 1% of the time, Pallas kernels for 0%

commit v1 on v0

v1 whole, which is shorter than its diff:
```python
import math

import jax
import jax.numpy as jnp
from jax import lax
from jax.experimental import pallas as pl
from jax.experimental.pallas import tpu as pltpu
from jax.sharding import PartitionSpec as P

HD = 128
CAP = 3
NX, NY, NZ = 4, 4, 8
MESH = pl.DeviceIdType.MESH
f32 = jnp.float32
bf16 = jnp.bfloat16


def place():
    section = lax.axis_index("section")
    enc = lax.axis_index("enc")
    x = lax.rem(enc, NX)
    y = lax.rem(section // 2, NY)
    z = (enc // NX) * 2 + section // (2 * NY)
    return x, y, z, lax.rem(section, 2)


def device(x, y, z, c):
    return (lax.rem(z, 2) * (2 * NY) + y * 2 + c, (z // 2) * NX + x)


def turn(a, d, n):
    return lax.rem(a + d + n, n)


class Links:
    def __init__(self, send_sem, recv_sem):
        self.send_sem, self.recv_sem = send_sem, recv_sem
        self.used = 0
        self.sent = []

    def send(self, src, dst, dev):
        i = self.used
        self.used += 1
        copy = pltpu.make_async_remote_copy(
            src_ref=src,
            dst_ref=dst,
            send_sem=self.send_sem.at[i],
            recv_sem=self.recv_sem.at[i],
            device_id=dev,
            device_id_type=MESH,
        )
        copy.start()
        self.sent.append(copy)
        return copy

    def finish(self):
        for copy in self.sent:
            copy.wait_send()


def enter(x, y, z, c):
    peers = [device(x, turn(y, d, NY), z, c) for d in (1, 2, 3)]
    peers += [device(turn(x, d, NX), y, z, c) for d in (1, -1)]
    peers += [device(x, y, turn(z, d, NZ), c) for d in (1, -1)]
    peers += [device(x, y, z, 1 - c)]
    barrier = pltpu.get_barrier_semaphore()
    for peer in peers:
        pl.semaphore_signal(barrier, inc=1, device_id=peer, device_id_type=MESH)
    pl.semaphore_wait(barrier, len(peers))


GATHER_SEMS = 160


def gather_kernel(
    own_ref, kw_ref, vw_ref, all_ref, kws_ref, vws_ref, held, column, rows, send_sem, recv_sem, local_sem
):
    x, y, z, c = place()
    links = Links(send_sem, recv_sem)
    right, left = device(turn(x, 1, NX), y, z, c), device(turn(x, -1, NX), y, z, c)
    up, down = device(x, y, turn(z, 1, NZ), c), device(x, y, turn(z, -1, NZ), c)
    other = device(x, y, z, 1 - c)
    enter(x, y, z, c)

    firsts = []
    for d in (1, 2, 3):
        firsts.append(links.send(own_ref, column.at[y], device(x, turn(y, d, NY), z, c)))
    weights = [links.send(kw_ref, kws_ref, other), links.send(vw_ref, vws_ref, other)]
    column[y] = own_ref[...]
    for copy in firsts:
        copy.wait_recv()
    half = own_ref.shape[-1]
    for p in range(CAP):
        for j in range(NY):
            rows[p, 4 * j : 4 * j + 4, :half] = column[j, p, 0:4, :]
            rows[p, 4 * j : 4 * j + 4, half:] = column[j, p, 4:8, :]
        held[p, x, z] = rows[p].astype(bf16)

    siblings, locals_ = [], []

    def keep(index):
        src = held.at[index]
        dst = all_ref.at[(c,) + index]
        siblings.append(links.send(src, dst, other))
        copy = pltpu.make_async_copy(src, dst, local_sem.at[len(locals_)])
        copy.start()
        locals_.append(copy)

    def ring(index, dev):
        return links.send(held.at[index], held.at[index], dev)

    both = pl.ds(0, 2)
    lo, hi = pl.ds(0, half), pl.ds(half, half)

    def x_start(zz):
        keep((both, x, zz))
        return zz, ring((both, x, zz), right), ring((both, x, zz), left)

    def x_next(state):
        zz, from_left, from_right = state
        from_left.wait_recv()
        a = ring((0, turn(x, -1, NX), zz), right)
        from_right.wait_recv()
        b = ring((1, turn(x, 1, NX), zz), left)
        keep((both, turn(x, -1, NX), zz))
        keep((both, turn(x, 1, NX), zz))
        return zz, a, b

    def x_end(state):
        zz, a, b = state
        a.wait_recv()
        b.wait_recv()
        keep((both, turn(x, 2, NX), zz))

    za = [(ring((both, x, z), up), ring((both, x, z), down))]
    xb = (ring((2, x, z), right), ring((2, x, z), left))
    stage1 = [[x_start(z)]]
    xb[0].wait_recv()
    xb2a = ring((2, turn(x, -1, NX), z, slice(None), lo), right)
    xb[1].wait_recv()
    xb2b = ring((2, turn(x, 1, NX), z, slice(None), hi), left)
    stage2 = []
    zb = None
    allx = slice(None)
    for s in (1, 2, 3, 4):
        below, above = turn(z, -s, NZ), turn(z, s, NZ)
        fa, fb = za[-1]
        fa.wait_recv()
        if s < 3:
            na = ring((both, x, below), up)
        elif s == 3:
            na = ring((0, x, below), up)
        fb.wait_recv()
        if s < 3:
            nb = ring((both, x, above), down)
        elif s == 3:
            nb = ring((1, x, above), down)
        if s < 4:
            za.append((na, nb))
            stage1.append([x_start(below), x_start(above)])
        else:
            stage1.append([x_start(below)])
        if s == 1:
            xb2a.wait_recv()
            xb2b.wait_recv()
            zb = (ring((2, allx, z), up), ring((2, allx, z), down))
            keep((2, allx, z))
        else:
            t = s - 1
            zb[0].wait_recv()
            na = ring((2, allx if t < 3 else pl.ds(0, 2), turn(z, -t, NZ)), up)
            zb[1].wait_recv()
            nb = ring((2, allx if t < 3 else pl.ds(2, 2), turn(z, t, NZ)), down)
            zb = (na, nb)
            keep((2, allx, turn(z, -t, NZ)))
            keep((2, allx, turn(z, t, NZ)))
        stage2.append([x_next(state) for state in stage1[s - 1]])
        if s >= 2:
            for state in stage2[s - 2]:
                x_end(state)
    stage2.append([x_next(state) for state in stage1[4]])
    for state in stage2[3] + stage2[4]:
        x_end(state)
    zb[0].wait_recv()
    zb[1].wait_recv()
    keep((2, allx, turn(z, 4, NZ)))

    for copy in weights + siblings:
        copy.wait_recv()
    for copy in locals_:
        copy.wait()
    links.finish()


def gather_latents(latents, key_weight, value_weight):
    width = latents.shape[2]
    stacked = latents.astype(f32).reshape(CAP, 4, 2, width // 2)
    stacked = stacked.transpose(0, 2, 1, 3).reshape(CAP, 8, width // 2)
    hbm = pl.BlockSpec(memory_space=pl.ANY)
    return pl.pallas_call(
        gather_kernel,
        name="gather_latents",
        out_shape=(
            jax.ShapeDtypeStruct((2, CAP, NX, NZ, 16, width), bf16),
            jax.ShapeDtypeStruct(key_weight.shape, bf16),
            jax.ShapeDtypeStruct(value_weight.shape, bf16),
        ),
        in_specs=[pl.BlockSpec(memory_space=pltpu.VMEM), hbm, hbm],
        out_specs=(hbm, hbm, hbm),
        scratch_shapes=[
            pltpu.VMEM((CAP, NX, NZ, 16, width), bf16),
            pltpu.VMEM((NY, CAP, 8, width // 2), f32),
            pltpu.VMEM((CAP, 16, width), f32),
            pltpu.SemaphoreType.DMA((GATHER_SEMS,)),
            pltpu.SemaphoreType.DMA((GATHER_SEMS,)),
            pltpu.SemaphoreType.DMA((64,)),
        ],
        compiler_params=pltpu.CompilerParams(
            collective_id=0, has_side_effects=True, vmem_limit_bytes=24 << 20
        ),
    )(stacked, key_weight, value_weight)


BLOCK = 128
GROUP = 8
CHUNK = 4


def attention_kernel(
    starts_ref, slot_ref, factor_ref, all_ref, q_ref, cot_ref, kw_ref, vw_ref,
    att_ref, gq_ref, gkv_ref, lat, keys, values, gacc, sem,
):
    images = slot_ref.shape[0]
    groups = images // GROUP
    group_rows = GROUP * 64
    tokens = q_ref.shape[0]
    heads = q_ref.shape[1] // HD
    hw = heads * HD
    scale = 1.0 / math.sqrt(HD)
    factor = factor_ref[0]

    def where_is(i):
        slot = slot_ref[i]
        enc = slot // CAP
        return slot - enc * CAP, lax.rem(enc, NX), enc // NX

    @pl.loop(0, images)
    def _(i):
        p, x, zh = where_is(i)
        for c in range(2):
            pltpu.make_async_copy(
                all_ref.at[c, p, x, pl.ds(2 * zh, 2)], lat.at[i, c], sem.at[i // GROUP]
            ).start()

    gkv_ref[...] = jnp.zeros_like(gkv_ref)
    for g in range(groups):
        rows = pl.ds(g * GROUP, GROUP)
        pltpu.make_async_copy(lat.at[rows], lat.at[rows], sem.at[g]).wait()
        data = lat[rows].reshape(group_rows, -1)
        out = pl.ds(g * group_rows, group_rows)
        keys[out, :] = jnp.dot(data, kw_ref[...], preferred_element_type=f32).astype(bf16)
        values[out, :] = jnp.dot(data, vw_ref[...], preferred_element_type=f32).astype(bf16)

    cols = CHUNK * 64
    nt = (((1,), (1,)), ((), ()))
    tn = (((0,), (0,)), ((), ()))

    @pl.loop(0, images // CHUNK)
    def _(q):
        edges = [starts_ref[q * CHUNK + j] for j in range(CHUNK + 1)]
        which = lax.broadcasted_iota(jnp.int32, (1, cols), 1) // 64
        first = jnp.full((1, cols), edges[0], jnp.int32)
        last = jnp.full((1, cols), edges[1], jnp.int32)
        for j in range(1, CHUNK):
            first = jnp.where(which == j, edges[j], first)
            last = jnp.where(which == j, edges[j + 1], last)
        krows = pl.ds(pl.multiple_of(q * cols, cols), cols)
        gacc[...] = jnp.zeros_like(gacc)

        @pl.loop(edges[0] // BLOCK, (edges[CHUNK] + BLOCK - 1) // BLOCK)
        def _(b):
            trows = pl.ds(pl.multiple_of(b * BLOCK, BLOCK), BLOCK)
            token = lax.broadcasted_iota(jnp.int32, (BLOCK, 1), 0) + b * BLOCK
            here = jnp.logical_and(token >= edges[0], token < edges[CHUNK])
            mask = jnp.logical_and(token >= first, token < last)
            for h in range(heads):
                hc = slice(h * HD, (h + 1) * HD)
                qb = q_ref[trows, hc]
                k = keys[krows, hc]
                v = values[krows, hc]
                gm = (factor * cot_ref[trows, hc].astype(f32)).astype(bf16)
                s = lax.dot_general(qb, k, nt, preferred_element_type=f32)
                gp = lax.dot_general(gm, v, nt, preferred_element_type=f32)
                s = jnp.where(mask, s * scale, -1e30)
                m = jnp.max(s, axis=1, keepdims=True)
                e = jnp.where(mask, jnp.exp(s - m), 0.0)
                total = jnp.sum(e, axis=1, keepdims=True)
                p = e * (1.0 / jnp.maximum(total, 1.0))
                pb = p.astype(bf16)
                w = jnp.sum(p * gp, axis=1, keepdims=True)
                gs = (p * (gp - w) * scale).astype(bf16)
                mix = jnp.dot(pb, v, preferred_element_type=f32)
                gq = jnp.dot(gs, k, preferred_element_type=f32)
                att_ref[trows, hc] = jnp.where(here, (factor * mix).astype(bf16), att_ref[trows, hc])
                gq_ref[trows, hc] = jnp.where(here, gq.astype(bf16), gq_ref[trows, hc])
                gacc[:, hc] += lax.dot_general(gs, qb, tn, preferred_element_type=f32)
                vc = slice(hw + h * HD, hw + (h + 1) * HD)
                gacc[:, vc] += lax.dot_general(pb, gm, tn, preferred_element_type=f32)

        for j in range(CHUNK):
            p, x, zh = where_is(q * CHUNK + j)
            for c in range(2):
                r = j * 64 + c * 32
                gkv_ref[c, p, x, pl.ds(2 * zh, 2)] = (
                    gacc[r : r + 32, :].astype(bf16).reshape(2, 16, 2 * hw)
                )


def attention(starts, image_slot, factor, everyone, queries, cotangent, key_weight, value_weight):
    tokens, hw = queries.shape
    width = key_weight.shape[0]
    images = image_slot.shape[0]
    vmem = pl.BlockSpec(memory_space=pltpu.VMEM)
    smem = pl.BlockSpec(memory_space=pltpu.SMEM)
    hbm = pl.BlockSpec(memory_space=pl.ANY)
    return pl.pallas_call(
        attention_kernel,
        name="attention",
        out_shape=(
            jax.ShapeDtypeStruct((tokens, hw), bf16),
            jax.ShapeDtypeStruct((tokens, hw), bf16),
            jax.ShapeDtypeStruct((2, CAP, NX, NZ, 16, 2 * hw), bf16),
        ),
        in_specs=[smem, smem, smem, hbm, vmem, vmem, vmem, vmem],
        out_specs=(vmem, vmem, vmem),
        scratch_shapes=[
            pltpu.VMEM((images, 2, 2, 16, width), bf16),
            pltpu.VMEM((images * 64, hw), bf16),
            pltpu.VMEM((images * 64, hw), bf16),
            pltpu.VMEM((CHUNK * 64, 2 * hw), f32),
            pltpu.SemaphoreType.DMA((images // GROUP,)),
        ],
        compiler_params=pltpu.CompilerParams(vmem_limit_bytes=40 << 20),
    )(starts, image_slot, factor, everyone, queries, cotangent, key_weight, value_weight)


SCATTER_SEMS = 80


def scatter_kernel(
    gkv_ref, kw_ref, vw_ref, kws_ref, vws_ref, out_ref,
    mine, theirs, part, xin, zin, xb_in, zb_in, col_out, col_in, total, send_sem, recv_sem, local_sem,
):
    x, y, z, c = place()
    links = Links(send_sem, recv_sem)
    right, left = device(turn(x, 1, NX), y, z, c), device(turn(x, -1, NX), y, z, c)
    up, down = device(x, y, turn(z, 1, NZ), c), device(x, y, turn(z, -1, NZ), c)
    other = device(x, y, z, 1 - c)
    hw = kw_ref.shape[1]
    width = kw_ref.shape[0]
    half = width // 2
    nt = (((1,), (1,)), ((), ()))
    enter(x, y, z, c)

    own = pltpu.make_async_copy(gkv_ref.at[c], mine, local_sem.at[0])
    own.start()
    pieces = []
    for k in (2, 1, -1, 0):
        xx = turn(x, k, NX)
        pieces.append(
            links.send(gkv_ref.at[1 - c, pl.ds(0, 2), xx], theirs.at[pl.ds(0, 2), xx], other)
        )
    piece_b = links.send(gkv_ref.at[1 - c, 2], theirs.at[2], other)
    own.wait()

    def project(a, b):
        r = lax.dot_general(a[:, :hw], kw_ref[...], nt, preferred_element_type=f32)
        r += lax.dot_general(a[:, hw:], vw_ref[...], nt, preferred_element_type=f32)
        r += lax.dot_general(b[:, :hw], kws_ref[...], nt, preferred_element_type=f32)
        r += lax.dot_general(b[:, hw:], vws_ref[...], nt, preferred_element_type=f32)
        return r.astype(bf16)

    def compute_a(i, k):
        pieces[i].wait_recv()
        xx = turn(x, k, NX)
        for p in range(2):
            a = mine[p, xx].reshape(NZ * 16, 2 * hw)
            b = theirs[p, xx].reshape(NZ * 16, 2 * hw)
            part[p, xx] = project(a, b).reshape(NZ, 16, width)

    def compute_b(xx):
        a = mine[2, xx].reshape(NZ * 16, 2 * hw)
        b = theirs[2, xx].reshape(NZ * 16, 2 * hw)
        part[2, xx] = project(a, b).reshape(NZ, 16, width)

    def plus(index, arrived):
        part[index] = (part[index].astype(f32) + arrived.astype(f32)).astype(bf16)

    compute_a(0, 2)
    far = turn(x, 2, NX)
    a1 = links.send(part.at[0, far], xin.at[0], right)
    b1 = links.send(part.at[1, far], xin.at[1], left)
    piece_b.wait_recv()
    for xx in range(NX):
        compute_b(xx)
    zf = turn(z, 4, NZ)
    zb = [
        links.send(part.at[2, pl.ds(0, 2), zf], zb_in.at[0, 0, pl.ds(0, 2)], up),
        links.send(part.at[2, pl.ds(2, 2), zf], zb_in.at[1, 0, pl.ds(2, 2)], down),
    ]
    compute_a(1, 1)
    compute_a(2, -1)
    xr, xl = turn(x, 1, NX), turn(x, -1, NX)
    a2 = links.send(part.at[1, xr], xin.at[2], right)
    b2 = links.send(part.at[0, xl], xin.at[3], left)
    compute_a(3, 0)

    def zb_step(s, zb):
        k = 4 - s
        zr, zl = turn(z, k, NZ), turn(z, -k, NZ)
        zb[0].wait_recv()
        if s == 1:
            for xx in (0, 1):
                plus((2, xx, zr), zb_in[0, 0, xx])
        else:
            for xx in range(NX):
                plus((2, xx, zr), zb_in[0, s - 1, xx])
        if k:
            n0 = links.send(part.at[2, :, zr], zb_in.at[0, s], up)
        zb[1].wait_recv()
        if s == 1:
            for xx in (2, 3):
                plus((2, xx, zl), zb_in[1, 0, xx])
        else:
            for xx in range(NX):
                plus((2, xx, zl), zb_in[1, s - 1, xx])
        if k:
            n1 = links.send(part.at[2, :, zl], zb_in.at[1, s], down)
            return [n0, n1]

    zb = zb_step(1, zb)
    a1.wait_recv()
    for zz in range(NZ):
        plus((0, xr, zz), xin[0, zz])
    a3 = links.send(part.at[0, xr], xin.at[4], right)
    b1.wait_recv()
    for zz in range(NZ):
        plus((1, xl, zz), xin[1, zz])
    b3 = links.send(part.at[1, xl], xin.at[5], left)
    zb = zb_step(2, zb)
    zb = zb_step(3, zb)
    a2.wait_recv()
    b2.wait_recv()
    for zz in range(NZ):
        plus((1, x, zz), xin[2, zz])
        plus((0, x, zz), xin[3, zz])
    zb_step(4, zb)
    xf = turn(x, 2, NX)
    c1 = links.send(part.at[2, xf, z, :, pl.ds(0, half)], xb_in.at[0], right)
    d1 = links.send(part.at[2, xf, z, :, pl.ds(half, half)], xb_in.at[1], left)
    c2 = links.send(part.at[2, xr, z, :, pl.ds(half, half)], xb_in.at[2], right)
    d2 = links.send(part.at[2, xl, z, :, pl.ds(0, half)], xb_in.at[3], left)
    a3.wait_recv()
    b3.wait_recv()
    for zz in range(NZ):
        plus((0, x, zz), xin[4, zz])
        plus((1, x, zz), xin[5, zz])
    za = [
        links.send(part.at[0, x, zf], zin.at[0, 0, 0], up),
        links.send(part.at[1, x, zf], zin.at[1, 0, 1], down),
    ]
    c1.wait_recv()
    cols = pl.ds(0, half)
    part[2, xr, z, :, cols] = (part[2, xr, z, :, cols].astype(f32) + xb_in[0].astype(f32)).astype(bf16)
    c3 = links.send(part.at[2, xr, z, :, pl.ds(0, half)], xb_in.at[4], right)
    d1.wait_recv()
    cols = pl.ds(half, half)
    part[2, xl, z, :, cols] = (part[2, xl, z, :, cols].astype(f32) + xb_in[1].astype(f32)).astype(bf16)
    d3 = links.send(part.at[2, xl, z, :, pl.ds(half, half)], xb_in.at[5], left)
    for s in (1, 2, 3):
        k = 4 - s
        zr, zl = turn(z, k, NZ), turn(z, -k, NZ)
        za[0].wait_recv()
        for p in (0,) if s == 1 else (0, 1):
            plus((p, x, zr), zin[0, s - 1, p])
        n0 = links.send(part.at[pl.ds(0, 2), x, zr], zin.at[0, s], up)
        za[1].wait_recv()
        for p in (1,) if s == 1 else (0, 1):
            plus((p, x, zl), zin[1, s - 1, p])
        n1 = links.send(part.at[pl.ds(0, 2), x, zl], zin.at[1, s], down)
        za = [n0, n1]
    za[0].wait_recv()
    za[1].wait_recv()
    for p in range(2):
        total[p] = part[p, x, z].astype(f32) + zin[0, 3, p].astype(f32) + zin[1, 3, p].astype(f32)
    for copy in (c2, d2, c3, d3):
        copy.wait_recv()
    last = part[2, x, z].astype(f32)
    total[2, :, :half] = last[:, :half] + xb_in[3].astype(f32) + xb_in[4].astype(f32)
    total[2, :, half:] = last[:, half:] + xb_in[2].astype(f32) + xb_in[5].astype(f32)

    for j in range(NY):
        for p in range(CAP):
            col_out[j, p, 0:4, :] = total[p, 4 * j : 4 * j + 4, :half]
            col_out[j, p, 4:8, :] = total[p, 4 * j : 4 * j + 4, half:]
    ends = []
    for d in (1, 2, 3):
        yy = turn(y, d, NY)
        ends.append(links.send(col_out.at[yy], col_in.at[d - 1], device(x, yy, z, c)))
    result = col_out[y]
    for d in range(3):
        ends[d].wait_recv()
        result = result + col_in[d]
    out_ref[...] = result
    links.finish()


def scatter_latents(gkv, kw, vw, kws, vws):
    width, hw = kw.shape
    half = width // 2
    vmem = pl.BlockSpec(memory_space=pltpu.VMEM)
    hbm = pl.BlockSpec(memory_space=pl.ANY)
    out = pl.pallas_call(
        scatter_kernel,
        name="scatter_latents",
        out_shape=jax.ShapeDtypeStruct((CAP, 8, half), f32),
        in_specs=[hbm, vmem, vmem, vmem, vmem],
        out_specs=vmem,
        scratch_shapes=[
            pltpu.VMEM((CAP, NX, NZ, 16, 2 * hw), bf16),
            pltpu.VMEM((CAP, NX, NZ, 16, 2 * hw), bf16),
            pltpu.VMEM((CAP, NX, NZ, 16, width), bf16),
            pltpu.VMEM((6, NZ, 16, width), bf16),
            pltpu.VMEM((2, 4, 2, 16, width), bf16),
            pltpu.VMEM((6, 16, half), bf16),
            pltpu.VMEM((2, 4, NX, 16, width), bf16),
            pltpu.VMEM((NY, CAP, 8, half), f32),
            pltpu.VMEM((NY - 1, CAP, 8, half), f32),
            pltpu.VMEM((CAP, 16, width), f32),
            pltpu.SemaphoreType.DMA((SCATTER_SEMS,)),
            pltpu.SemaphoreType.DMA((SCATTER_SEMS,)),
            pltpu.SemaphoreType.DMA((1,)),
        ],
        compiler_params=pltpu.CompilerParams(
            collective_id=1, has_side_effects=True, vmem_limit_bytes=48 << 20
        ),
    )(gkv, kw, vw, kws, vws)
    return out.reshape(CAP, 2, 4, half).transpose(0, 2, 1, 3).reshape(CAP, 4, width)


def image_slots(image_counts, images):
    image_ends = jnp.cumsum(image_counts)
    image_starts = image_ends - image_counts
    index = jnp.arange(images, dtype=jnp.int32)
    owner = jnp.sum((index[:, None] >= image_ends[None, :]).astype(jnp.int32), axis=1)
    match = owner[:, None] == jnp.arange(image_counts.shape[0], dtype=jnp.int32)[None, :]
    first = jnp.sum(jnp.where(match, image_starts[None, :], 0), axis=1)
    return owner * CAP + index - first


def on_device(
    latents, key_weight, value_weight, gate_logit, queries, cotangent, image_counts, token_image
):
    images = 2 * image_counts.shape[0]
    kw, vw = key_weight[0], value_weight[0]
    image_slot = image_slots(image_counts, images).astype(jnp.int32)
    edge = jnp.arange(images + 1, dtype=jnp.int32)
    starts = jnp.sum((token_image[None, :] < edge[:, None]).astype(jnp.int32), axis=1)
    factor = jnp.tanh(gate_logit)
    everyone, kws, vws = gather_latents(latents, kw, vw)
    attended, grad_queries, gkv = attention(
        starts, image_slot, factor, everyone, queries[0], cotangent[0], kw, vw
    )
    grad_latents = scatter_latents(gkv, kw, vw, kws, vws)
    return attended[None], grad_queries[None], grad_latents


def solution(mesh):
    shards = P("section", None, "enc")
    return jax.shard_map(
        on_device,
        mesh=mesh,
        in_specs=(
            P("enc", "section", None), shards, shards, P("section"), shards, shards, P(), P(),
        ),
        out_specs=(shards, shards, P("enc", "section", None)),
        check_vma=False,
    )
```

time: 692 us -> 141 us (0.20)
  waiting for transfers between devices: 343 us -> 0 us
  local copies, waits for them, and re-layouts: 169 us -> 7.84 us
  matrix products: 128 us -> 0 us
  Pallas kernels: 0 us -> 127 us
  blocking collectives: 19.9 us -> 0 us
  between operations: 15.3 us -> 1.39 us
    pallas_call x0 -> x3, Pallas kernels: none -> 127 us  [the longest x1 51.8 us: scatter_latents(): pl.pallas_call(scatter_kernel, name='scatter_latents', out_shape=jax.Shap...]
    reduce_scatter x1 -> x0, waiting for transfers between devices: 127 us -> none  [on_device(): lax.psum_scatter(lax.dot_general(in_slots, weights, (((in_slots.ndim - 1,...]
    unnamed x4 -> x0, waiting for transfers between devices: 117 us -> none
    dot_general x42 -> x0, matrix products: 115 us -> none  [the longest x8 31.4 us: one_block(): jnp.einsum('hts,shd->thd', grad_scores, key_band, preferred_element_type=...]
    dynamic_update_slice x40 -> x0, local copies, waits for them, and re-layouts: 104 us -> none  [the longest x8 44.6 us: one_block(): lax.dynamic_update_slice_in_dim(grad_keys, key_part, first_row, 0)]
    all_gather x1 -> x0, waiting for transfers between devices: 99.3 us -> none  [on_device(): shard_piece = lax.all_gather(gathered, 'enc', axis=0, tiled=True)]
    dynamic_slice x40 -> x0, local copies, waits for them, and re-layouts: 34.7 us -> none  [the longest x24 19.8 us: on_device(): lax.scan(one_block, (zeros, zeros), block_inputs)]
    all_gather x1 -> x0, blocking collectives: 19.9 us -> none  [on_device(): gathered = lax.all_gather(latents, 'section', axis=1, tiled=True)]
  transfers between devices with their start and end apart: 3 -> 0, of which waited for: 3 -> 0; matrix products, arithmetic and copies ran while one was open for 1% -> 0% of each run, Pallas kernels for 0% -> 0%
where the time goes in v1:
time: 141 us; the launch traced here: 139 us
  Pallas kernels  127 us (90%)
  local copies, waits for them, and re-layouts  7.84 us (6%)
  other arithmetic  2.57 us (2%)
    pallas_call x1, Pallas kernels, scatter_latents(): pl.pallas_call(scatter_kernel, name='scatter_latents', out_shape=jax.Shap...  51.8 us
    pallas_call x1, Pallas kernels, gather_latents(): pl.pallas_call(gather_kernel, name='gather_latents', out_shape=(jax.Shape...  45.2 us
    pallas_call x1, Pallas kernels, attention(): pl.pallas_call(attention_kernel, name='attention', out_shape=(jax.ShapeDt...  30.3 us
    unnamed x16, local copies, waits for them, and re-layouts  6.43 us

profile of v1, /device:TPU:8, one launch (start us, length us, event | category | flops | bytes accessed | tf_op | source)
XLA Modules:
  0.0 139.1 jit_solution(1227543750767444147)
XLA Ops:
  1.3 0.8 convert_reduce_fusion.starts_ref
  2.1 0.7 copy.17
  2.9 0.1 reduce
  3.0 0.1 convert_reduce_fusion.1
  3.1 0.7 sub.6
  3.8 0.1 select_reduce_fusion
  3.9 0.8 convert_bitcast_fusion
  4.7 0.0 copy-start
  4.7 1.1 copy-done
  5.8 0.0 copy-start.3
  5.8 1.1 copy-done.3
  6.8 0.0 copy-start.2
  6.8 0.0 copy-start.5
  6.8 45.2 %gather_latents.1 = (bf16[2,3,4,8,16,1280]{5,4,3,2,1,0:T(8,128)(2,1)S(1)}, bf16[1280,256]{1,0:T(8,128)(2,1)S(1)}, bf16[1280,256]{1,0:T(8,128)(2,1)S(1)}) custom-call(f32[3,8,640]{2,1,0:T(8,128)S(1)} %reshape.55.own_ref, bf16[1280,256]{1,0:T(8,128)(2,1)S(1)} %bitcast.14, bf16[1280,256]{1,0:T(8,128)(2,1)S(1)} %bitcast.17), custom_call_target="tpu_custom_call" | custom-call | tf_op jit(solution)/shard_map/gather_latents/pallas_call | solution.py:200
  52.1 0.0 copy-start.1
  52.1 1.1 copy-done.1
  53.2 1.1 copy-done.4
  54.2 1.0 copy-done.6
  55.3 1.0 copy-done.7
  56.3 30.3 %attention.1 = (bf16[1024,256]{1,0:T(8,128)(2,1)}, bf16[1024,256]{1,0:T(8,128)(2,1)}, bf16[2,3,4,8,16,512]{5,4,3,2,1,0:T(8,128)(2,1)S(1)}) custom-call(s32[33]{0:T(128)S(1)} %convert_reduce_fusion.starts_ref, s32[32]{0:T(128)S(1)} %add_subtract_fusion.slot_ref, f32[1]{0:T(128)S(6)} %tanh.3.factor_ref, ...), custom_call_target="tpu_custom_call" | custom-call | tf_op jit(solution)/shard_map/attention/pallas_call | solution.py:326
  86.7 0.0 copy-done.2
  86.7 0.0 copy-done.5
  86.7 51.8 %scatter_latents.1 = f32[3,8,640]{2,1,0:T(8,128)S(1)} custom-call(bf16[2,3,4,8,16,512]{5,4,3,2,1,0:T(8,128)(2,1)S(1)} %get-tuple-element.12.gkv_ref, bf16[1280,256]{1,0:T(8,128)(2,1)S(1)} %bitcast.16, bf16[1280,256]{1,0:T(8,128)(2,1)S(1)} %bitcast.19, bf16[1280,256]{1,0:T(8,128)(2,1)S(1)} %get-tuple-element.13.kws_ref, ...), custom_call_target="tpu_custom_call" | custom-call | tf_op jit(solution)/shard_map/scatter_latents/pallas_call | solution.py:523
  138.5 0.6 reshape.52
  (6 shorter events, 0.1 us)
Async XLA Ops:
  4.7 1.1 copy-start
  5.8 1.1 copy-start.3
  6.8 79.8 %copy-start.2 = (bf16[1,1280,256]{2,1,0:T(8,128)(2,1)S(1)}, bf16[1,1280,256]{2,1,0:T(8,128)(2,1)}, u32[]{:S(2)}) copy-start(bf16[1,1280,256]{2,1,0:T(8,128)(2,1)} %param.9) | copy-start | bytes 1966084
  6.8 79.9 %copy-start.5 = (bf16[1,1280,256]{2,1,0:T(8,128)(2,1)S(1)}, bf16[1,1280,256]{2,1,0:T(8,128)(2,1)}, u32[]{:S(2)}) copy-start(bf16[1,1280,256]{2,1,0:T(8,128)(2,1)} %param.10) | copy-start | bytes 1966084
  52.1 1.1 copy-start.1
  53.2 1.1 copy-start.4
  54.2 1.0 copy-start.6
  55.3 1.0 copy-start.7

commit v2 on v0

v2 whole, which is shorter than its diff:
```python
import math

import jax
import jax.numpy as jnp
from jax import lax
from jax.experimental import pallas as pl
from jax.experimental.pallas import tpu as pltpu
from jax.sharding import PartitionSpec as P

HD = 128
CAP = 3
NX, NY, NZ = 4, 4, 8
MESH = pl.DeviceIdType.MESH
f32 = jnp.float32
bf16 = jnp.bfloat16


def place():
    section = lax.axis_index("section")
    enc = lax.axis_index("enc")
    x = lax.rem(enc, NX)
    y = lax.rem(section // 2, NY)
    z = (enc // NX) * 2 + section // (2 * NY)
    return x, y, z, lax.rem(section, 2)


def device(x, y, z, c):
    return (lax.rem(z, 2) * (2 * NY) + y * 2 + c, (z // 2) * NX + x)


def turn(a, d, n):
    return lax.rem(a + d + n, n)


class Links:
    def __init__(self, send_sem, recv_sem):
        self.send_sem, self.recv_sem = send_sem, recv_sem
        self.used = 0
        self.sent = []

    def send(self, src, dst, dev):
        i = self.used
        self.used += 1
        copy = pltpu.make_async_remote_copy(
            src_ref=src,
            dst_ref=dst,
            send_sem=self.send_sem.at[i],
            recv_sem=self.recv_sem.at[i],
            device_id=dev,
            device_id_type=MESH,
        )
        copy.start()
        self.sent.append(copy)
        return copy

    def finish(self):
        for copy in self.sent:
            copy.wait_send()


def greet(x, y, z, c):
    peers = [device(x, turn(y, d, NY), z, c) for d in (1, 2, 3)]
    peers += [device(turn(x, d, NX), y, z, c) for d in (1, 2, 3)]
    peers += [device(x, y, turn(z, d, NZ), c) for d in (1, -1, 2, -2)]
    peers += [device(x, y, z, 1 - c)]
    barrier = pltpu.get_barrier_semaphore()
    for peer in peers:
        pl.semaphore_signal(barrier, inc=1, device_id=peer, device_id_type=MESH)


def meet():
    pl.semaphore_wait(pltpu.get_barrier_semaphore(), NX + NY + 3)


GATHER_SEMS = 160
XCUT, YCUT = 640, 1152
QUARTER = (YCUT - XCUT) // NY


def gather_kernel(
    own_hbm, kw_ref, vw_ref, kv_ref, kws_ref, vws_ref,
    hx, hy, hz, own, mine, column, rows, kw, vw, kv, send_sem, recv_sem, local_sem,
):
    x, y, z, c = place()
    links = Links(send_sem, recv_sem)
    right, left = device(turn(x, 1, NX), y, z, c), device(turn(x, -1, NX), y, z, c)
    north, south = device(x, turn(y, 1, NY), z, c), device(x, turn(y, -1, NY), z, c)
    along = {d: device(x, y, turn(z, d, NZ), c) for d in (-2, -1, 1, 2)}
    other = device(x, y, z, 1 - c)
    width = own_hbm.shape[-1]
    hw = kw_ref.shape[-1]
    greet(x, y, z, c)
    first = pltpu.make_async_copy(own_hbm, own, local_sem.at[2])
    first.start()
    loads = [
        pltpu.make_async_copy(kw_ref, kw, local_sem.at[0]),
        pltpu.make_async_copy(vw_ref, vw, local_sem.at[1]),
    ]
    for copy in loads:
        copy.start()
    first.wait()
    for p in range(CAP):
        mine[4 * p : 4 * p + 4, :] = own[p].astype(f32)
    mine[12:16, :] = jnp.zeros((4, width), f32)
    column[y] = mine[...].astype(bf16)
    meet()

    firsts = []
    for d in (1, 3, 2):
        firsts.append(links.send(column.at[y], column.at[y], device(x, turn(y, d, NY), z, c)))

    for copy in firsts:
        copy.wait_recv()
    for j in range(NY):
        block = column[j].astype(f32)
        for p in range(CAP):
            rows[p, 4 * j : 4 * j + 4, :] = block[4 * p : 4 * p + 4, :]
    part = pl.ds(pl.multiple_of(XCUT + y * QUARTER, 128), QUARTER)
    hx[c, z, x] = rows[:, :, :XCUT].astype(bf16)
    hy[c, z, y, x] = rows[:, :, part].astype(bf16)
    hz[c, z, x] = rows[:, :, YCUT:].astype(bf16)

    def send(ref, dev):
        return links.send(ref, ref, dev)

    def arrive(*copies):
        for copy in copies:
            copy.wait_recv()

    stores = []

    def project(zz):
        n = 2 * NX * CAP * 16
        data = [hx[:, zz].reshape(n, XCUT)]
        data += [hy[:, zz, j].reshape(n, QUARTER) for j in range(NY)]
        data += [hz[:, zz].reshape(n, width - YCUT)]
        data = jnp.concatenate(data, axis=1)
        for w, cols in ((kw, slice(0, hw)), (vw, slice(hw, 2 * hw))):
            r = jnp.dot(data, w[...], preferred_element_type=f32).astype(bf16)
            kv[:, zz, :, :, :, cols] = r.reshape(2, NX, CAP, 16, hw)
        copy = pltpu.make_async_copy(kv.at[:, zz], kv_ref.at[:, zz], local_sem.at[3 + len(stores)])
        copy.start()
        stores.append(copy)

    x1, x3 = turn(x, 1, NX), turn(x, -1, NX)
    y1, y3 = turn(y, 1, NY), turn(y, -1, NY)
    xpeers = [device(turn(x, d, NX), y, z, c) for d in (1, 3, 2)]
    few, many = pl.ds(0, 1), pl.ds(1, 2)
    front, back = pl.ds(0, 2), pl.ds(2, 2)

    class Last:
        def __init__(self, axis, k):
            self.axis, self.k, self.zz = axis, k, turn(z, k, NZ)
            if axis == 0:
                self.go = [send(hx.at[c, self.zz, x], dev) for dev in (right, left)]
            else:
                self.go = [send(hy.at[c, self.zz, y], dev) for dev in (north, south)]

        def forward(self):
            a, b = self.go
            if self.axis == 0:
                sa, sb = (few, many) if self.k % 2 else (many, few)
                arrive(a)
                a = send(hx.at[c, self.zz, x3, sa], right)
                arrive(b)
                b = send(hx.at[c, self.zz, x1, sb], left)
            else:
                arrive(a)
                a = send(hy.at[c, self.zz, y3, front], north)
                arrive(b)
                b = send(hy.at[c, self.zz, y1, back], south)
            self.go = [a, b]

        def end(self):
            arrive(*self.go)
            self.kept = send((hx if self.axis == 0 else hy).at[c, self.zz], other)

    def block(axis, k, cut=None):
        zz = turn(z, k, NZ)
        ref = hx.at[c, zz, x] if axis == 0 else hy.at[c, zz, y]
        return ref if cut is None else ref.at[cut]

    def over_z(axis):
        return {d: send(block(axis, 0), along[d]) for d in (1, -1, 2, -2)}

    def over_z_again(axis, go):
        go2 = {}
        cut = (few, many) if axis == 0 else (pl.ds(0, 3), pl.ds(3, 1))
        for d, s in ((2, 0), (-2, 1)):
            arrive(go[d])
            go2[3 * d // 2] = send(block(axis, -d), along[d // 2])
            go2[2 * d] = send(block(axis, -d, cut[s]), along[d])
        return go2

    y_first = [send(hy.at[c, z, y, x], dev) for dev in xpeers]
    go_x = over_z(0)
    z_first = [send(hz.at[c, z, x], dev) for dev in xpeers]
    last = {(0, 0): Last(0, 0)}
    arrive(*y_first)
    go_y = over_z(1)
    last[1, 0] = Last(1, 0)
    arrive(*z_first)
    go_z = [send(hz.at[c, z], along[1]), send(hz.at[c, z], along[-1])]
    zkept = {0: send(hz.at[c, z], other)}
    weights = [links.send(kw_ref, kws_ref, other), links.send(vw_ref, vws_ref, other)]

    def ring_z(s):
        out = []
        for i, d in ((0, -s), (1, s)):
            zz = turn(z, d, NZ)
            arrive(go_z[i])
            if s < 3:
                out.append(send(hz.at[c, zz], along[1 - 2 * i]))
            elif s == 3:
                out.append(send(hz.at[c, zz, (front, back)[i]], along[1 - 2 * i]))
            if s < 4 or i:
                zkept[d] = send(hz.at[c, zz], other)
        return out

    def finish(k):
        arrive(last[0, k].kept, last[1, k].kept, zkept[k])
        project(turn(z, k, NZ))

    for copy in loads:
        copy.wait()
    for d in (1, -1):
        arrive(go_x[d])
        last[0, -d] = Last(0, -d)
    far_x = over_z_again(0, go_x)
    for d in (2, -2):
        last[0, d] = Last(0, d)
    last[0, 0].forward()
    for d in (1, -1):
        arrive(go_y[d])
        last[1, -d] = Last(1, -d)
    far_y = over_z_again(1, go_y)
    for d in (2, -2):
        last[1, d] = Last(1, d)
    last[1, 0].forward()
    go_z = ring_z(1)
    for d in (1, -1):
        last[0, d].forward()
    for d in (3, -3):
        arrive(far_x[d])
        last[0, -d] = Last(0, -d)
    arrive(far_x[4], far_x[-4])
    last[0, 4] = Last(0, 4)
    for d in (1, -1):
        last[1, d].forward()
    for d in (3, -3):
        arrive(far_y[d])
        last[1, -d] = Last(1, -d)
    arrive(far_y[4], far_y[-4])
    last[1, 4] = Last(1, 4)
    go_z = ring_z(2)
    last[0, 0].end()
    last[1, 0].end()
    for d in (2, -2):
        last[0, d].forward()
        last[1, d].forward()
    for d in (1, -1):
        last[0, d].end()
        last[1, d].end()
    finish(0)
    go_z = ring_z(3)
    for d in (3, -3):
        last[0, d].forward()
        last[1, d].forward()
    last[0, 4].forward()
    last[1, 4].forward()
    for d in (2, -2):
        last[0, d].end()
        last[1, d].end()
    finish(1)
    finish(-1)
    ring_z(4)
    for d in (3, -3):
        last[0, d].end()
        last[1, d].end()
    finish(2)
    finish(-2)
    last[0, 4].end()
    last[1, 4].end()
    finish(3)
    finish(-3)
    finish(4)

    arrive(*weights)
    for copy in stores:
        copy.wait()
    links.finish()


def gather_latents(latents, key_weight, value_weight):
    width = latents.shape[2]
    hw = key_weight.shape[1]
    hbm = pl.BlockSpec(memory_space=pltpu.HBM)
    return pl.pallas_call(
        gather_kernel,
        name="gather_latents",
        out_shape=(
            jax.ShapeDtypeStruct((2, NZ, NX, CAP, 16, 2 * hw), bf16),
            jax.ShapeDtypeStruct(key_weight.shape, bf16),
            jax.ShapeDtypeStruct(value_weight.shape, bf16),
        ),
        in_specs=[hbm, hbm, hbm],
        out_specs=(hbm, hbm, hbm),
        scratch_shapes=[
            pltpu.VMEM((2, NZ, NX, CAP, 16, XCUT), bf16),
            pltpu.VMEM((2, NZ, NY, NX, CAP, 16, QUARTER), bf16),
            pltpu.VMEM((2, NZ, NX, CAP, 16, width - YCUT), bf16),
            pltpu.VMEM(latents.shape, bf16),
            pltpu.VMEM((16, width), f32),
            pltpu.VMEM((NY, 16, width), bf16),
            pltpu.VMEM((CAP, 16, width), f32),
            pltpu.VMEM(key_weight.shape, bf16),
            pltpu.VMEM(value_weight.shape, bf16),
            pltpu.VMEM((2, NZ, NX, CAP, 16, 2 * hw), bf16),
            pltpu.SemaphoreType.DMA((GATHER_SEMS,)),
            pltpu.SemaphoreType.DMA((GATHER_SEMS,)),
            pltpu.SemaphoreType.DMA((12,)),
        ],
        compiler_params=pltpu.CompilerParams(
            collective_id=0, has_side_effects=True, vmem_limit_bytes=62 << 20
        ),
    )(latents, key_weight, value_weight)


BLOCK = 128
CHUNK = 4
SIDE = 4


def attention_kernel(
    counts_ref, gate_ref, token_ref, kv_ref, q_hbm, cot_hbm,
    att_hbm, gq_hbm, gkv_ref,
    kvs, stage, zeros, q_ref, cot_ref, att_ref, gq_ref, gacc,
    slots, starts, chunk_of, block_of, begin_of, sem, io_sem,
):
    owners = counts_ref.shape[0]
    images = 2 * owners
    chunks = images // CHUNK
    heads = q_ref.shape[1] // HD
    hw = heads * HD
    scale = 1.0 / math.sqrt(HD)
    cols = CHUNK * 64
    tokens = q_ref.shape[0]
    pairs = chunk_of.shape[0]
    nt = (((1,), (1,)), ((), ()))

    copies = [
        pltpu.make_async_copy(q_hbm, q_ref, io_sem.at[0]),
        pltpu.make_async_copy(cot_hbm, cot_ref, io_sem.at[1]),
        pltpu.make_async_copy(att_ref, att_hbm, io_sem.at[4]),
        pltpu.make_async_copy(gq_ref, gq_hbm, io_sem.at[5]),
    ]
    zeros[...] = jnp.zeros_like(zeros)
    n = 0
    for e in range(owners):
        count = counts_ref[e]
        x, zs = e % NX, pl.ds(2 * (e // NX), 2)
        for p in range(CAP):

            @pl.when(p < count)
            def _():
                slots[n + p] = e * CAP + p
                for c in range(2):
                    pltpu.make_async_copy(
                        kv_ref.at[c, zs, x, p], kvs.at[n + p, c], sem.at[0]
                    ).start()

            @pl.when(p >= count)
            def _():
                for c in range(2):
                    pltpu.make_async_copy(zeros, gkv_ref.at[c, zs, x, p], io_sem.at[2]).start()

        n = n + count
        if e == 1:
            copies[0].start()
            copies[1].start()
    token_image = token_ref[...]
    for i in range(images + 1):
        starts[i] = jnp.sum((token_image < i).astype(jnp.int32))
    factor = jnp.tanh(jnp.full((1, HD), gate_ref[0], f32))
    for i in range(pairs):
        chunk_of[i] = 0
        block_of[i] = 0
        begin_of[i] = tokens
    n = 0
    for q in range(chunks):
        b0 = starts[q * CHUNK] // BLOCK
        b1 = (starts[(q + 1) * CHUNK] + BLOCK - 1) // BLOCK

        @pl.loop(b0, b1)
        def _(b):
            i = n + b - b0
            chunk_of[i] = q
            block_of[i] = b
            begin_of[i] = b * BLOCK

        n = n + b1 - b0
    gacc[...] = jnp.zeros_like(gacc)
    copies[0].wait()
    copies[1].wait()
    pltpu.make_async_copy(kvs, kvs, sem.at[0]).wait()

    @pl.loop(0, (n + SIDE - 1) // SIDE)
    def _(step):
        work = []
        for u in range(SIDE):
            i = step * SIDE + u
            q, b, begin = chunk_of[i], block_of[i], begin_of[i]
            four = pl.ds(q * CHUNK, CHUNK)
            trows = pl.ds(pl.multiple_of(b * BLOCK, BLOCK), BLOCK)
            krows = pl.ds(pl.multiple_of(q * cols, cols), cols)
            edges = [starts[q * CHUNK + j] for j in range(CHUNK + 1)]
            which = lax.broadcasted_iota(jnp.int32, (1, cols), 1) // 64
            first = jnp.full((1, cols), edges[0], jnp.int32)
            last = jnp.full((1, cols), edges[1], jnp.int32)
            for j in range(1, CHUNK):
                first = jnp.where(which == j, edges[j], first)
                last = jnp.where(which == j, edges[j + 1], last)
            token = lax.broadcasted_iota(jnp.int32, (BLOCK, 1), 0) + begin
            here = jnp.logical_and(token >= edges[0], token < edges[CHUNK])
            wide = jnp.logical_and(token >= first, token < last).astype(f32).astype(bf16)
            lane = lax.broadcasted_iota(jnp.int32, (1, BLOCK), 1) + begin
            tall = [
                jnp.logical_and(lane >= edges[j], lane < edges[j + 1]) for j in range(CHUNK)
            ]
            ones = [t.astype(f32).astype(bf16) for t in tall]
            for h in range(heads):
                hc = slice(h * HD, (h + 1) * HD)
                vc = slice(hw + h * HD, hw + (h + 1) * HD)
                qb = q_ref[trows, hc]
                k = kvs[four, :, :, :, hc].reshape(cols, HD)
                v = kvs[four, :, :, :, vc].reshape(cols, HD)
                gm = (factor * cot_ref[trows, hc].astype(f32)).astype(bf16)
                s = lax.dot_general(k, qb, nt, preferred_element_type=f32)
                gp = lax.dot_general(v, gm, nt, preferred_element_type=f32)
                work.append((hc, vc, trows, krows, here, wide, tall, ones, qb, k, v, gm, s, gp))

        def pick(full, tall):
            out = full[(CHUNK - 1) * 64 :]
            for j in range(CHUNK - 1):
                out = jnp.where(tall[j], full[j * 64 : (j + 1) * 64], out)
            return out

        def spread(small, ones, wide):
            rows = small.astype(bf16)
            down = jnp.concatenate([rows * ones[j] for j in range(CHUNK)], axis=0)
            twice = jnp.concatenate([small, small], axis=0).T.astype(bf16)
            return down, jnp.concatenate([twice] * (CHUNK // 2), axis=1) * wide

        done = []
        for hc, vc, trows, krows, here, wide, tall, ones, qb, k, v, gm, s, gp in work:
            s = pick(s, tall)
            gp = pick(gp, tall)
            e = jnp.exp((s - jnp.max(s, axis=0, keepdims=True)) * scale)
            p = e * (1.0 / jnp.sum(e, axis=0, keepdims=True))
            w = jnp.sum(p * gp, axis=0, keepdims=True)
            gs = p * (gp - w) * scale
            p_down, p_wide = spread(p, ones, wide)
            gs_down, gs_wide = spread(gs, ones, wide)
            done.append((
                jnp.dot(p_wide, v, preferred_element_type=f32),
                jnp.dot(gs_wide, k, preferred_element_type=f32),
                jnp.dot(gs_down, qb, preferred_element_type=f32),
                jnp.dot(p_down, gm, preferred_element_type=f32),
            ))
        for item, (mix, gq, gk, gv) in zip(work, done):
            hc, vc, trows, krows, here = item[:5]
            att_ref[trows, hc] = jnp.where(here, (factor * mix).astype(bf16), att_ref[trows, hc])
            gq_ref[trows, hc] = jnp.where(here, gq.astype(bf16), gq_ref[trows, hc])
            gacc[krows, hc] += gk
            gacc[krows, vc] += gv

    copies[2].start()
    copies[3].start()

    @pl.loop(0, chunks)
    def _(q):
        krows = pl.ds(pl.multiple_of(q * cols, cols), cols)
        stage[pl.ds(q * CHUNK, CHUNK)] = (
            gacc[krows, :].astype(bf16).reshape(CHUNK, 2, 2, 16, 2 * hw)
        )
        for j in range(CHUNK):
            i = q * CHUNK + j
            slot = slots[i]
            enc = slot // CAP
            for c in range(2):
                pltpu.make_async_copy(
                    stage.at[i, c],
                    gkv_ref.at[c, pl.ds(2 * (enc // NX), 2), lax.rem(enc, NX), slot - enc * CAP],
                    io_sem.at[3],
                ).start()

    empty = stage.at[pl.ds(0, CAP * owners - images)]
    pltpu.make_async_copy(empty, empty, io_sem.at[2]).wait()
    pltpu.make_async_copy(stage, stage, io_sem.at[3]).wait()
    copies[2].wait()
    copies[3].wait()


def attention(image_counts, gate_logit, token_image, kv, queries, cotangent):
    tokens, hw = queries.shape
    images = 2 * image_counts.shape[0]
    pairs = images // CHUNK + tokens // BLOCK
    vmem = pl.BlockSpec(memory_space=pltpu.VMEM)
    smem = pl.BlockSpec(memory_space=pltpu.SMEM)
    hbm = pl.BlockSpec(memory_space=pltpu.HBM)
    return pl.pallas_call(
        attention_kernel,
        name="attention",
        out_shape=(
            jax.ShapeDtypeStruct((tokens, hw), bf16),
            jax.ShapeDtypeStruct((tokens, hw), bf16),
            jax.ShapeDtypeStruct((2, NZ, NX, CAP, 16, 2 * hw), bf16),
        ),
        in_specs=[smem, smem, vmem, hbm, hbm, hbm],
        out_specs=(hbm, hbm, hbm),
        scratch_shapes=[
            pltpu.VMEM((images, 2, 2, 16, 2 * hw), bf16),
            pltpu.VMEM((images, 2, 2, 16, 2 * hw), bf16),
            pltpu.VMEM((2, 16, 2 * hw), bf16),
            pltpu.VMEM((tokens, hw), bf16),
            pltpu.VMEM((tokens, hw), bf16),
            pltpu.VMEM((tokens, hw), bf16),
            pltpu.VMEM((tokens, hw), bf16),
            pltpu.VMEM((images * 64, 2 * hw), f32),
            pltpu.SMEM((images,), jnp.int32),
            pltpu.SMEM((images + 1,), jnp.int32),
            pltpu.SMEM((pairs,), jnp.int32),
            pltpu.SMEM((pairs,), jnp.int32),
            pltpu.SMEM((pairs,), jnp.int32),
            pltpu.SemaphoreType.DMA((1,)),
            pltpu.SemaphoreType.DMA((6,)),
        ],
        compiler_params=pltpu.CompilerParams(vmem_limit_bytes=62 << 20),
    )(image_counts, gate_logit, token_image.reshape(8, tokens // 8), kv, queries, cotangent)


SCATTER_SEMS = 128


def scatter_kernel(
    gkv_ref, kw_hbm, vw_hbm, kws_hbm, vws_hbm, out_ref,
    weights, mine, theirs, px, py, pz, rx1, rx2, ry1, ry2, zx, zx4, zy, zy4, rz, ty, tz, ly, lz,
    total, col, col_out, col_in, send_sem, recv_sem, local_sem,
):
    x, y, z, c = place()
    links = Links(send_sem, recv_sem)
    right, left = device(turn(x, 1, NX), y, z, c), device(turn(x, -1, NX), y, z, c)
    north, south = device(x, turn(y, 1, NY), z, c), device(x, turn(y, -1, NY), z, c)
    along = {d: device(x, y, turn(z, d, NZ), c) for d in (-2, -1, 1, 2)}
    other = device(x, y, z, 1 - c)
    hw = kw_hbm.shape[1]
    width = kw_hbm.shape[0]
    rest = width - YCUT
    nt = (((1,), (1,)), ((), ()))
    greet(x, y, z, c)
    loads = [pltpu.make_async_copy(gkv_ref.at[c], mine, local_sem.at[0])]
    for i, ref in enumerate((kw_hbm, vw_hbm, kws_hbm, vws_hbm)):
        loads.append(pltpu.make_async_copy(ref, weights.at[i], local_sem.at[1 + i]))
    for copy in loads:
        copy.start()
    meet()
    order = (4, 3, -3, 2, -2, 1, -1, 0)
    at = {k: turn(z, k, NZ) for k in order}
    pieces = {k: links.send(gkv_ref.at[1 - c, at[k]], theirs.at[at[k]], other) for k in order}
    for copy in loads:
        copy.wait()

    def arrive(*copies):
        for copy in copies:
            copy.wait_recv()

    def plus(ref, *arrived):
        value = ref[...].astype(f32)
        for item in arrived:
            value = value + item.astype(f32)
        ref[...] = value.astype(bf16)

    x1, x3, x2 = turn(x, 1, NX), turn(x, -1, NX), turn(x, 2, NX)
    y1, y3, y2 = turn(y, 1, NY), turn(y, -1, NY), turn(y, 2, NY)
    few, many = pl.ds(0, 1), pl.ds(1, 2)
    front, back = pl.ds(0, 2), pl.ds(2, 2)
    n = NX * CAP * 16

    def project(*ks):
        arrive(*[pieces[k] for k in ks])
        data = [ref[at[k]].reshape(n, 2 * hw) for ref in (mine, theirs) for k in ks]
        if len(ks) > 1:
            data = [jnp.concatenate(data[:2], axis=0), jnp.concatenate(data[2:], axis=0)]
        r = None
        for i in range(4):
            a = data[i // 2][:, (i % 2) * hw : (i % 2 + 1) * hw]
            t = lax.dot_general(a, weights[i], nt, preferred_element_type=f32)
            r = t if r is None else r + t
        r = r.astype(bf16)
        for i, k in enumerate(ks):
            part = r[i * n : (i + 1) * n]
            px[at[k]] = part[:, :XCUT].reshape(NX, CAP, 16, XCUT)
            for j in range(NY):
                py[at[k], j] = part[:, XCUT + j * QUARTER : XCUT + (j + 1) * QUARTER].reshape(
                    NX, CAP, 16, QUARTER
                )
            pz[at[k]] = part[:, YCUT:].reshape(NX, CAP, 16, rest)

    class First:
        def __init__(self, axis, k):
            self.axis, self.k, self.i = axis, k, order.index(k)
            zz = at[k]
            if axis == 0:
                self.cuts = (few, many) if k % 2 else (many, few)
                self.part, self.near, self.far = px.at[zz], (x1, x3), x2
                self.r1, self.r2, self.own = rx1, rx2, x
                self.devs = (right, left)
            else:
                self.cuts = (front, back)
                self.part, self.near, self.far = py.at[zz], (y1, y3), y2
                self.r1, self.r2, self.own = ry1, ry2, y
                self.devs = (north, south)
            self.go = [
                links.send(
                    self.part.at[self.far, self.cuts[s]],
                    self.r1.at[self.i, s, pl.ds(0, self.cuts[s].size)],
                    self.devs[s],
                )
                for s in (0, 1)
            ]

        def forward(self):
            go = []
            for s in (0, 1):
                arrive(self.go[s])
                plus(
                    self.part.at[self.near[s], self.cuts[s]],
                    self.r1[self.i, s, pl.ds(0, self.cuts[s].size)],
                )
                go.append(
                    links.send(self.part.at[self.near[s]], self.r2.at[self.i, s], self.devs[s])
                )
            self.go = go

        def end(self):
            arrive(*self.go)
            plus(self.part.at[self.own], self.r2[self.i, 0], self.r2[self.i, 1])

    def block(axis, k, cut=None):
        ref = px.at[at[k], x] if axis == 0 else py.at[at[k], y]
        return ref if cut is None else ref.at[cut]

    def zcuts(axis):
        return (few, many) if axis == 0 else (pl.ds(0, 3), pl.ds(3, 1))

    def z_far(axis):
        land, land4 = (zx, zx4) if axis == 0 else (zy, zy4)
        cuts = zcuts(axis)
        go = []
        for s, d in ((0, 1), (1, -1)):
            near = links.send(block(axis, 3 * d), land.at[0, s], along[d])
            cut = cuts[1 - s]
            wide = links.send(
                block(axis, 4, cut), land4.at[s, pl.ds(0, cut.size)], along[2 * d]
            )
            go.append((near, wide))
        return go

    def z_mid(axis, go):
        land, land4 = (zx, zx4) if axis == 0 else (zy, zy4)
        cuts = zcuts(axis)
        out = []
        for s, d in ((0, 1), (1, -1)):
            near, wide = go[s]
            arrive(near)
            plus(block(axis, 2 * d), land[0, s])
            cut = cuts[1 - s]
            arrive(wide)
            plus(block(axis, 2 * d, cut), land4[s, pl.ds(0, cut.size)])
            out.append(links.send(block(axis, 2 * d), land.at[1, s], along[2 * d]))
        return out

    def z_near(axis):
        land = zx if axis == 0 else zy
        return [
            links.send(block(axis, d), land.at[2, s], along[d]) for s, d in ((0, 1), (1, -1))
        ]

    def z_sum(axis):
        land = zx if axis == 0 else zy
        value = block(axis, 0)[...].astype(f32)
        for i in (1, 2):
            for s in (0, 1):
                value = value + land[i, s].astype(f32)
        return value

    def z_ring(step, go):
        k = 4 - step
        out = []
        for s, d in ((0, 1), (1, -1)):
            cut = (front, back)[s] if step == 1 else pl.ds(0, NX)
            arrive(go[s])
            plus(pz.at[at[k * d], cut], rz[s, step - 1, cut])
            if k:
                out.append(links.send(pz.at[at[k * d]], rz.at[s, step], along[d]))
        return out

    def over_x(value, mine_ref, land):
        mine_ref[...] = value.astype(bf16)
        go = []
        for i, d in enumerate((1, 3, 2)):
            xx = turn(x, d, NX)
            go.append(links.send(mine_ref.at[xx], land.at[i], device(xx, y, z, c)))
        return go

    first = {}

    def begin(*ks):
        for k in ks:
            for axis in (0, 1):
                first[axis, k] = First(axis, k)

    def forward(*ks):
        for k in ks:
            for axis in (0, 1):
                first[axis, k].forward()

    def end(*ks):
        for axis in (0, 1):
            for k in ks:
                first[axis, k].end()

    project(4)
    begin(4)
    go_z = [
        links.send(pz.at[at[4], front], rz.at[0, 0, front], along[1]),
        links.send(pz.at[at[4], back], rz.at[1, 0, back], along[-1]),
    ]
    project(3, -3)
    begin(3, -3)
    forward(4)
    project(2, -2)
    begin(2, -2)
    go_z = z_ring(1, go_z)
    forward(3, -3)
    end(4)
    project(1, -1)
    begin(1, -1)
    go_z = z_ring(2, go_z)
    end(3, -3)
    far_x, far_y = z_far(0), z_far(1)
    forward(2, -2)
    project(0)
    begin(0)
    go_z = z_ring(3, go_z)
    end(2, -2)
    forward(1, -1)
    mid_y = z_mid(1, far_y)
    mid_x = z_mid(0, far_x)
    z_ring(4, go_z)
    end_z = over_x(pz[z].astype(f32), lz, tz)
    forward(0)
    end(1, -1)
    near_y, near_x = z_near(1), z_near(0)
    end(0)
    arrive(*mid_y, *near_y)
    end_y = over_x(z_sum(1), ly, ty)
    arrive(*mid_x, *near_x)
    total[:, :, :XCUT] = z_sum(0)
    arrive(*end_z)
    value = lz[x].astype(f32)
    for i in range(3):
        value = value + tz[i].astype(f32)
    total[:, :, XCUT + QUARTER :] = value
    arrive(*end_y)
    value = ly[x].astype(f32)
    for i in range(3):
        value = value + ty[i].astype(f32)
    total[:, :, XCUT : XCUT + QUARTER] = value

    for j in range(NY):
        for p in range(CAP):
            col[j, 4 * p : 4 * p + 4, :] = total[p, 4 * j : 4 * j + 4, :]
        col[j, 12:16, :] = jnp.zeros((4, total.shape[-1]), f32)
        col_out[j] = col[j].astype(bf16)
    ends = []
    for i, d in enumerate((1, 3, 2)):
        yy = turn(y, d, NY)
        ends.append(links.send(col_out.at[yy], col_in.at[i], device(x, yy, z, c)))
    result = col[y]

    def quarter(j):
        return pl.ds(pl.multiple_of(XCUT + j * QUARTER, 128), QUARTER)

    for p in range(CAP):
        out_ref[p, :, quarter(y)] = result[4 * p : 4 * p + 4, XCUT : XCUT + QUARTER]
    for i, d in enumerate((1, 3, 2)):
        arrive(ends[i])
        got = col_in[i].astype(f32)
        for p in range(CAP):
            out_ref[p, :, quarter(turn(y, -d, NY))] = got[4 * p : 4 * p + 4, XCUT : XCUT + QUARTER]
        result = result + got
    for p in range(CAP):
        out_ref[p, :, :XCUT] = result[4 * p : 4 * p + 4, :XCUT]
        out_ref[p, :, YCUT:] = result[4 * p : 4 * p + 4, XCUT + QUARTER :]
    links.finish()


def scatter_latents(gkv, kw, vw, kws, vws):
    width, hw = kw.shape
    rest = width - YCUT
    last = XCUT + QUARTER + rest
    hbm = pl.BlockSpec(memory_space=pltpu.HBM)

    def buffer(*shape):
        return pltpu.VMEM(shape, bf16)

    return pl.pallas_call(
        scatter_kernel,
        name="scatter_latents",
        out_shape=jax.ShapeDtypeStruct((CAP, 4, width), f32),
        in_specs=[hbm, hbm, hbm, hbm, hbm],
        out_specs=pl.BlockSpec(memory_space=pltpu.VMEM),
        scratch_shapes=[
            buffer(4, width, hw),
            buffer(NZ, NX, CAP, 16, 2 * hw),
            buffer(NZ, NX, CAP, 16, 2 * hw),
            buffer(NZ, NX, CAP, 16, XCUT),
            buffer(NZ, NY, NX, CAP, 16, QUARTER),
            buffer(NZ, NX, CAP, 16, rest),
            buffer(NZ, 2, 2, 16, XCUT),
            buffer(NZ, 2, CAP, 16, XCUT),
            buffer(NZ, 2, 2, CAP, 16, QUARTER),
            buffer(NZ, 2, NX, CAP, 16, QUARTER),
            buffer(3, 2, CAP, 16, XCUT),
            buffer(2, 2, 16, XCUT),
            buffer(3, 2, NX, CAP, 16, QUARTER),
            buffer(2, 3, CAP, 16, QUARTER),
            buffer(2, 4, NX, CAP, 16, rest),
            buffer(3, CAP, 16, QUARTER),
            buffer(3, CAP, 16, rest),
            buffer(NX, CAP, 16, QUARTER),
            buffer(NX, CAP, 16, rest),
            pltpu.VMEM((CAP, 16, last), f32),
            pltpu.VMEM((NY, 16, last), f32),
            buffer(NY, 16, last),
            buffer(3, 16, last),
            pltpu.SemaphoreType.DMA((SCATTER_SEMS,)),
            pltpu.SemaphoreType.DMA((SCATTER_SEMS,)),
            pltpu.SemaphoreType.DMA((5,)),
        ],
        compiler_params=pltpu.CompilerParams(
            collective_id=1, has_side_effects=True, vmem_limit_bytes=62 << 20
        ),
    )(gkv, kw, vw, kws, vws)


def on_device(
    latents, key_weight, value_weight, gate_logit, queries, cotangent, image_counts, token_image
):
    kw, vw = key_weight[0], value_weight[0]
    kv, kws, vws = gather_latents(latents, kw, vw)
    attended, grad_queries, gkv = attention(
        image_counts, gate_logit, token_image, kv, queries[0], cotangent[0]
    )
    grad_latents = scatter_latents(gkv, kw, vw, kws, vws)
    return attended[None], grad_queries[None], grad_latents


def solution(mesh):
    shards = P("section", None, "enc")
    return jax.shard_map(
        on_device,
        mesh=mesh,
        in_specs=(
            P("enc", "section", None), shards, shards, P("section"), shards, shards, P(), P(),
        ),
        out_specs=(shards, shards, P("enc", "section", None)),
        check_vma=False,
    )
```

time: 692 us -> 96.6 us (0.14); the launches traced: 684 us -> 96.4 us
  waiting for transfers between devices: 343 us -> 0 us
  local copies, waits for them, and re-layouts: 169 us -> 1.46 us
  matrix products: 128 us -> 0 us
  Pallas kernels: 0 us -> 93.6 us
  blocking collectives: 19.9 us -> 0 us
  between operations: 15.3 us -> 1.3 us
  other arithmetic: 8.22 us -> 0 us
    reduce_scatter x1 -> x0, waiting for transfers between devices: 127 us -> none  [on_device(): lax.psum_scatter(lax.dot_general(in_slots, weights, (((in_slots.ndim - 1,...]
    unnamed x4 -> x0, waiting for transfers between devices: 117 us -> none
    dot_general x42 -> x0, matrix products: 115 us -> none  [the longest x8 31.4 us: one_block(): jnp.einsum('hts,shd->thd', grad_scores, key_band, preferred_element_type=...]
    dynamic_update_slice x40 -> x0, local copies, waits for them, and re-layouts: 104 us -> none  [the longest x8 44.6 us: one_block(): lax.dynamic_update_slice_in_dim(grad_keys, key_part, first_row, 0)]
    all_gather x1 -> x0, waiting for transfers between devices: 99.3 us -> none  [on_device(): shard_piece = lax.all_gather(gathered, 'enc', axis=0, tiled=True)]
    pallas_call x0 -> x3, Pallas kernels: none -> 93.6 us  [the longest x1 42.3 us: scatter_latents(): pl.pallas_call(scatter_kernel, name='scatter_latents', out_shape=jax.Shap...]
    dynamic_slice x40 -> x0, local copies, waits for them, and re-layouts: 34.7 us -> none  [the longest x24 19.8 us: on_device(): lax.scan(one_block, (zeros, zeros), block_inputs)]
    all_gather x1 -> x0, blocking collectives: 19.9 us -> none  [on_device(): gathered = lax.all_gather(latents, 'section', axis=1, tiled=True)]
  transfers between devices with their start and end apart: 3 -> 0, of which waited for: 3 -> 0; matrix products, arithmetic and copies ran while one was open for 1% -> 0% of each run, Pallas kernels for 0% -> 0%
where the time goes in v2:
time: 96.6 us; the launch traced here: 96.4 us
  Pallas kernels  93.6 us (97%)
  local copies, waits for them, and re-layouts  1.46 us (2%)
  between operations  1.3 us (1%)
    pallas_call x1, Pallas kernels, scatter_latents(): pl.pallas_call(scatter_kernel, name='scatter_latents', out_shape=jax.Shap...  42.3 us
    pallas_call x1, Pallas kernels, gather_latents(): pl.pallas_call(gather_kernel, name='gather_latents', out_shape=(jax.Shape...  42.1 us
    pallas_call x1, Pallas kernels, attention(): pl.pallas_call(attention_kernel, name='attention', out_shape=(jax.ShapeDt...  9.21 us

profile of v2, /device:TPU:8, one launch (start us, length us, event | category | flops | bytes accessed | tf_op | source)
XLA Modules:
  0.0 96.4 jit_solution(18235385377040278858)
XLA Ops:
  1.3 42.1 %gather_latents.1 = (bf16[2,8,4,3,16,512]{5,4,3,2,1,0:T(8,128)(2,1)}, bf16[1280,256]{1,0:T(8,128)(2,1)}, bf16[1280,256]{1,0:T(8,128)(2,1)}) custom-call(bf16[3,4,1280]{2,1,0:T(4,128)(2,1)} %own_hbm.1, bf16[1280,256]{1,0:T(8,128)(2,1)} %bitcast.7, bf16[1280,256]{1,0:T(8,128)(2,1)} %bitcast.9), custom_call_target="tpu_custom_call" | custom-call | tf_op jit(solution)/shard_map/gather_latents/pallas_call | solution.py:298
  43.4 9.2 %attention.1 = (bf16[1024,256]{1,0:T(8,128)(2,1)}, bf16[1024,256]{1,0:T(8,128)(2,1)}, bf16[2,8,4,3,16,512]{5,4,3,2,1,0:T(8,128)(2,1)}) custom-call(s32[16]{0:T(128)} %counts_ref.1, f32[1]{0:T(128)S(6)} %copy.12.gate_ref, s32[8,128]{1,0:T(8,128)} %bitcast.13, bf16[2,8,4,3,16,512]{5,4,3,2,1,0:T(8,128)(2,1)} %get-tuple-element.9.kv_ref, ...), custom_call_target="tpu_custom_call" | custom-call | tf_op jit(solution)/shard_map/attention/pallas_call | solution.py:511
  52.6 42.3 %scatter_latents.1 = f32[3,4,1280]{2,1,0:T(4,128)} custom-call(bf16[2,8,4,3,16,512]{5,4,3,2,1,0:T(8,128)(2,1)} %get-tuple-element.12.gkv_ref, bf16[1280,256]{1,0:T(8,128)(2,1)} %bitcast.8, bf16[1280,256]{1,0:T(8,128)(2,1)} %bitcast.10, bf16[1280,256]{1,0:T(8,128)(2,1)} %get-tuple-element.13.kws_hbm, bf16[1280,256]{1,0:T(8,128)(2,1)} %get-tuple-element.14.vws_hbm), custom_call_target="tpu_custom_call" | custom-call | tf_op jit(solution)/shard_map/scatter_latents/pallas_call | solution.py:818
  94.9 1.5 %copy.13 = f32[3,4,1280]{2,1,0:T(4,128)} copy(f32[3,4,1280]{2,1,0:T(4,128)} %scatter_latents.1) | data formatting | bytes 122880

commit v3 on v2

--- a/solution.py
+++ b/solution.py
@@ -61,7 +61,7 @@
 def greet(x, y, z, c):
     peers = [device(x, turn(y, d, NY), z, c) for d in (1, 2, 3)]
     peers += [device(turn(x, d, NX), y, z, c) for d in (1, 2, 3)]
-    peers += [device(x, y, turn(z, d, NZ), c) for d in (1, -1, 2, -2)]
+    peers += [device(x, y, turn(z, d, NZ), c) for d in (1, -1)]
     peers += [device(x, y, z, 1 - c)]
     barrier = pltpu.get_barrier_semaphore()
     for peer in peers:
@@ -69,23 +69,22 @@
 
 
 def meet():
-    pl.semaphore_wait(pltpu.get_barrier_semaphore(), NX + NY + 3)
+    pl.semaphore_wait(pltpu.get_barrier_semaphore(), NX + NY + 1)
 
 
 GATHER_SEMS = 160
-XCUT, YCUT = 640, 1152
-QUARTER = (YCUT - XCUT) // NY
+XCUT, YCUT, QUARTER = 640, 1152, 128
 
 
 def gather_kernel(
-    own_hbm, kw_ref, vw_ref, kv_ref, kws_ref, vws_ref,
-    hx, hy, hz, own, mine, column, rows, kw, vw, kv, send_sem, recv_sem, local_sem,
+    own_hbm, kw_ref, vw_ref, kv_ref, theirs_ref,
+    hx, hy, hz, own, mine, column, rows, weights, kv, kv_out, send_sem, recv_sem, local_sem,
 ):
     x, y, z, c = place()
     links = Links(send_sem, recv_sem)
     right, left = device(turn(x, 1, NX), y, z, c), device(turn(x, -1, NX), y, z, c)
     north, south = device(x, turn(y, 1, NY), z, c), device(x, turn(y, -1, NY), z, c)
-    along = {d: device(x, y, turn(z, d, NZ), c) for d in (-2, -1, 1, 2)}
+    along = {d: device(x, y, turn(z, d, NZ), c) for d in (-1, 1)}
     other = device(x, y, z, 1 - c)
     width = own_hbm.shape[-1]
     hw = kw_ref.shape[-1]
@@ -93,8 +92,8 @@
     first = pltpu.make_async_copy(own_hbm, own, local_sem.at[2])
     first.start()
     loads = [
-        pltpu.make_async_copy(kw_ref, kw, local_sem.at[0]),
-        pltpu.make_async_copy(vw_ref, vw, local_sem.at[1]),
+        pltpu.make_async_copy(kw_ref, weights.at[0], local_sem.at[0]),
+        pltpu.make_async_copy(vw_ref, weights.at[1], local_sem.at[1]),
     ]
     for copy in loads:
         copy.start()
@@ -116,9 +115,9 @@
         for p in range(CAP):
             rows[p, 4 * j : 4 * j + 4, :] = block[4 * p : 4 * p + 4, :]
     part = pl.ds(pl.multiple_of(XCUT + y * QUARTER, 128), QUARTER)
-    hx[c, z, x] = rows[:, :, :XCUT].astype(bf16)
-    hy[c, z, y, x] = rows[:, :, part].astype(bf16)
-    hz[c, z, x] = rows[:, :, YCUT:].astype(bf16)
+    hx[z, x] = rows[:, :, :XCUT].astype(bf16)
+    hy[z, y, x] = rows[:, :, part].astype(bf16)
+    hz[z, x] = rows[:, :, YCUT:].astype(bf16)
 
     def send(ref, dev):
         return links.send(ref, ref, dev)
@@ -128,19 +127,36 @@
             copy.wait_recv()
 
     stores = []
-
-    def project(zz):
-        n = 2 * NX * CAP * 16
-        data = [hx[:, zz].reshape(n, XCUT)]
-        data += [hy[:, zz, j].reshape(n, QUARTER) for j in range(NY)]
-        data += [hz[:, zz].reshape(n, width - YCUT)]
-        data = jnp.concatenate(data, axis=1)
-        for w, cols in ((kw, slice(0, hw)), (vw, slice(hw, 2 * hw))):
-            r = jnp.dot(data, w[...], preferred_element_type=f32).astype(bf16)
-            kv[:, zz, :, :, :, cols] = r.reshape(2, NX, CAP, 16, hw)
-        copy = pltpu.make_async_copy(kv.at[:, zz], kv_ref.at[:, zz], local_sem.at[3 + len(stores)])
+    swaps = {}
+
+    def store(i, zz):
+        j = 3 + len(stores)
+        copy = pltpu.make_async_copy(kv.at[i, zz], kv_ref.at[i, zz], local_sem.at[j])
         copy.start()
         stores.append(copy)
+
+    def project(zz):
+        n = NX * CAP * 16
+        data = [hx[zz].reshape(n, XCUT)]
+        data += [hy[zz, j].reshape(n, QUARTER) for j in range(NY)]
+        data += [hz[zz].reshape(n, width - YCUT)]
+        data = jnp.concatenate(data, axis=1)
+        for i in (2, 3, 0, 1):
+            r = jnp.dot(data, weights[i], preferred_element_type=f32).astype(bf16)
+            r = r.reshape(NX, CAP, 16, hw)
+            cols = slice((i % 2) * hw, (i % 2 + 1) * hw)
+            if i < 2:
+                kv[c, zz, :, :, :, cols] = r
+            else:
+                kv_out[zz, :, :, :, cols] = r
+            if i == 3:
+                swaps[len(swaps)] = zz, links.send(kv_out.at[zz], kv.at[c, zz], other)
+        store(c, zz)
+
+    def swapped(i):
+        zz, copy = swaps[i]
+        copy.wait_recv()
+        store(1 - c, zz)
 
     x1, x3 = turn(x, 1, NX), turn(x, -1, NX)
     y1, y3 = turn(y, 1, NY), turn(y, -1, NY)
@@ -152,140 +168,112 @@
         def __init__(self, axis, k):
             self.axis, self.k, self.zz = axis, k, turn(z, k, NZ)
             if axis == 0:
-                self.go = [send(hx.at[c, self.zz, x], dev) for dev in (right, left)]
+                self.go = [send(hx.at[self.zz, x], dev) for dev in (right, left)]
             else:
-                self.go = [send(hy.at[c, self.zz, y], dev) for dev in (north, south)]
+                self.go = [send(hy.at[self.zz, y], dev) for dev in (north, south)]
 
         def forward(self):
             a, b = self.go
             if self.axis == 0:
                 sa, sb = (few, many) if self.k % 2 else (many, few)
                 arrive(a)
-                a = send(hx.at[c, self.zz, x3, sa], right)
+                a = send(hx.at[self.zz, x3, sa], right)
                 arrive(b)
-                b = send(hx.at[c, self.zz, x1, sb], left)
+                b = send(hx.at[self.zz, x1, sb], left)
             else:
                 arrive(a)
-                a = send(hy.at[c, self.zz, y3, front], north)
+                a = send(hy.at[self.zz, y3, front], north)
                 arrive(b)
-                b = send(hy.at[c, self.zz, y1, back], south)
+                b = send(hy.at[self.zz, y1, back], south)
             self.go = [a, b]
 
         def end(self):
             arrive(*self.go)
-            self.kept = send((hx if self.axis == 0 else hy).at[c, self.zz], other)
 
     def block(axis, k, cut=None):
         zz = turn(z, k, NZ)
-        ref = hx.at[c, zz, x] if axis == 0 else hy.at[c, zz, y]
+        ref = (hx.at[zz, x], hy.at[zz, y], hz.at[zz])[axis]
         return ref if cut is None else ref.at[cut]
 
     def over_z(axis):
-        return {d: send(block(axis, 0), along[d]) for d in (1, -1, 2, -2)}
-
-    def over_z_again(axis, go):
-        go2 = {}
-        cut = (few, many) if axis == 0 else (pl.ds(0, 3), pl.ds(3, 1))
-        for d, s in ((2, 0), (-2, 1)):
-            arrive(go[d])
-            go2[3 * d // 2] = send(block(axis, -d), along[d // 2])
-            go2[2 * d] = send(block(axis, -d, cut[s]), along[d])
-        return go2
-
-    y_first = [send(hy.at[c, z, y, x], dev) for dev in xpeers]
+        return [send(block(axis, 0), along[1]), send(block(axis, 0), along[-1])]
+
+    def pass_on(axis, s, go):
+        cuts = ((few, many), (pl.ds(0, 3), pl.ds(3, 1)), (front, back))[axis]
+        out = []
+        for i, d in ((0, -s), (1, s)):
+            arrive(go[i])
+            if s < 4:
+                out.append(send(block(axis, d, cuts[i] if s == 3 else None), along[1 - 2 * i]))
+        if axis < 2:
+            for d in (-s, s) if s < 4 else (4,):
+                last[axis, d] = Last(axis, d)
+        return out
+
+    for copy in loads:
+        copy.wait()
+    y_first = [send(hy.at[z, y, x], dev) for dev in xpeers]
+    z_first = [send(hz.at[z, x], dev) for dev in xpeers]
     go_x = over_z(0)
-    z_first = [send(hz.at[c, z, x], dev) for dev in xpeers]
+    swap_w = [links.send(weights.at[i], weights.at[2 + i], other) for i in (0, 1)]
     last = {(0, 0): Last(0, 0)}
     arrive(*y_first)
     go_y = over_z(1)
     last[1, 0] = Last(1, 0)
     arrive(*z_first)
-    go_z = [send(hz.at[c, z], along[1]), send(hz.at[c, z], along[-1])]
-    zkept = {0: send(hz.at[c, z], other)}
-    weights = [links.send(kw_ref, kws_ref, other), links.send(vw_ref, vws_ref, other)]
-
-    def ring_z(s):
-        out = []
-        for i, d in ((0, -s), (1, s)):
-            zz = turn(z, d, NZ)
-            arrive(go_z[i])
-            if s < 3:
-                out.append(send(hz.at[c, zz], along[1 - 2 * i]))
-            elif s == 3:
-                out.append(send(hz.at[c, zz, (front, back)[i]], along[1 - 2 * i]))
-            if s < 4 or i:
-                zkept[d] = send(hz.at[c, zz], other)
-        return out
+    go_z = over_z(2)
 
     def finish(k):
-        arrive(last[0, k].kept, last[1, k].kept, zkept[k])
         project(turn(z, k, NZ))
 
-    for copy in loads:
-        copy.wait()
-    for d in (1, -1):
-        arrive(go_x[d])
-        last[0, -d] = Last(0, -d)
-    far_x = over_z_again(0, go_x)
-    for d in (2, -2):
-        last[0, d] = Last(0, d)
-    last[0, 0].forward()
-    for d in (1, -1):
-        arrive(go_y[d])
-        last[1, -d] = Last(1, -d)
-    far_y = over_z_again(1, go_y)
-    for d in (2, -2):
-        last[1, d] = Last(1, d)
-    last[1, 0].forward()
-    go_z = ring_z(1)
-    for d in (1, -1):
-        last[0, d].forward()
-    for d in (3, -3):
-        arrive(far_x[d])
-        last[0, -d] = Last(0, -d)
-    arrive(far_x[4], far_x[-4])
-    last[0, 4] = Last(0, 4)
-    for d in (1, -1):
-        last[1, d].forward()
-    for d in (3, -3):
-        arrive(far_y[d])
-        last[1, -d] = Last(1, -d)
-    arrive(far_y[4], far_y[-4])
-    last[1, 4] = Last(1, 4)
-    go_z = ring_z(2)
-    last[0, 0].end()
-    last[1, 0].end()
-    for d in (2, -2):
-        last[0, d].forward()
-        last[1, d].forward()
-    for d in (1, -1):
-        last[0, d].end()
-        last[1, d].end()
+    arrive(*swap_w)
+    theirs = pltpu.make_async_copy(weights.at[pl.ds(2, 2)], theirs_ref, local_sem.at[2])
+    theirs.start()
+
+    def forward(*ks):
+        for axis in (0, 1):
+            for k in ks:
+                last[axis, k].forward()
+
+    def end(*ks):
+        for axis in (0, 1):
+            for k in ks:
+                last[axis, k].end()
+
+    go_x = pass_on(0, 1, go_x)
+    go_y = pass_on(1, 1, go_y)
+    go_z = pass_on(2, 1, go_z)
+    forward(0)
+    go_x = pass_on(0, 2, go_x)
+    go_y = pass_on(1, 2, go_y)
+    go_z = pass_on(2, 2, go_z)
+    forward(1, -1)
+    end(0)
+    go_x = pass_on(0, 3, go_x)
+    go_y = pass_on(1, 3, go_y)
+    go_z = pass_on(2, 3, go_z)
+    forward(2, -2)
     finish(0)
-    go_z = ring_z(3)
-    for d in (3, -3):
-        last[0, d].forward()
-        last[1, d].forward()
-    last[0, 4].forward()
-    last[1, 4].forward()
-    for d in (2, -2):
-        last[0, d].end()
-        last[1, d].end()
+    end(1, -1)
+    pass_on(0, 4, go_x)
+    pass_on(1, 4, go_y)
+    pass_on(2, 4, go_z)
     finish(1)
+    forward(3, -3)
     finish(-1)
-    ring_z(4)
-    for d in (3, -3):
-        last[0, d].end()
-        last[1, d].end()
+    end(2, -2)
+    forward(4)
     finish(2)
     finish(-2)
-    last[0, 4].end()
-    last[1, 4].end()
+    end(3, -3)
     finish(3)
     finish(-3)
+    end(4)
     finish(4)
 
-    arrive(*weights)
+    for i in range(NZ):
+        swapped(i)
+    theirs.wait()
     for copy in stores:
         copy.wait()
     links.finish()
@@ -300,25 +288,24 @@
         name="gather_latents",
         out_shape=(
             jax.ShapeDtypeStruct((2, NZ, NX, CAP, 16, 2 * hw), bf16),
-            jax.ShapeDtypeStruct(key_weight.shape, bf16),
-            jax.ShapeDtypeStruct(value_weight.shape, bf16),
+            jax.ShapeDtypeStruct((2,) + key_weight.shape, bf16),
         ),
         in_specs=[hbm, hbm, hbm],
-        out_specs=(hbm, hbm, hbm),
+        out_specs=(hbm, hbm),
         scratch_shapes=[
-            pltpu.VMEM((2, NZ, NX, CAP, 16, XCUT), bf16),
-            pltpu.VMEM((2, NZ, NY, NX, CAP, 16, QUARTER), bf16),
-            pltpu.VMEM((2, NZ, NX, CAP, 16, width - YCUT), bf16),
+            pltpu.VMEM((NZ, NX, CAP, 16, XCUT), bf16),
+            pltpu.VMEM((NZ, NY, NX, CAP, 16, QUARTER), bf16),
+            pltpu.VMEM((NZ, NX, CAP, 16, width - YCUT), bf16),
             pltpu.VMEM(latents.shape, bf16),
             pltpu.VMEM((16, width), f32),
             pltpu.VMEM((NY, 16, width), bf16),
             pltpu.VMEM((CAP, 16, width), f32),
-            pltpu.VMEM(key_weight.shape, bf16),
-            pltpu.VMEM(value_weight.shape, bf16),
+            pltpu.VMEM((4,) + key_weight.shape, bf16),
             pltpu.VMEM((2, NZ, NX, CAP, 16, 2 * hw), bf16),
+            pltpu.VMEM((NZ, NX, CAP, 16, 2 * hw), bf16),
             pltpu.SemaphoreType.DMA((GATHER_SEMS,)),
             pltpu.SemaphoreType.DMA((GATHER_SEMS,)),
-            pltpu.SemaphoreType.DMA((12,)),
+            pltpu.SemaphoreType.DMA((3 + 2 * NZ,)),
         ],
         compiler_params=pltpu.CompilerParams(
             collective_id=0, has_side_effects=True, vmem_limit_bytes=62 << 20
@@ -364,15 +351,11 @@
             @pl.when(p < count)
             def _():
                 slots[n + p] = e * CAP + p
-                for c in range(2):
-                    pltpu.make_async_copy(
-                        kv_ref.at[c, zs, x, p], kvs.at[n + p, c], sem.at[0]
-                    ).start()
+                pltpu.make_async_copy(kv_ref.at[:, zs, x, p], kvs.at[n + p], sem.at[0]).start()
 
             @pl.when(p >= count)
             def _():
-                for c in range(2):
-                    pltpu.make_async_copy(zeros, gkv_ref.at[c, zs, x, p], io_sem.at[2]).start()
+                pltpu.make_async_copy(zeros, gkv_ref.at[:, zs, x, p], io_sem.at[2]).start()
 
         n = n + count
         if e == 1:
@@ -487,12 +470,11 @@
             i = q * CHUNK + j
             slot = slots[i]
             enc = slot // CAP
-            for c in range(2):
-                pltpu.make_async_copy(
-                    stage.at[i, c],
-                    gkv_ref.at[c, pl.ds(2 * (enc // NX), 2), lax.rem(enc, NX), slot - enc * CAP],
-                    io_sem.at[3],
-                ).start()
+            pltpu.make_async_copy(
+                stage.at[i],
+                gkv_ref.at[:, pl.ds(2 * (enc // NX), 2), lax.rem(enc, NX), slot - enc * CAP],
+                io_sem.at[3],
+            ).start()
 
     empty = stage.at[pl.ds(0, CAP * owners - images)]
     pltpu.make_async_copy(empty, empty, io_sem.at[2]).wait()
@@ -521,7 +503,7 @@
         scratch_shapes=[
             pltpu.VMEM((images, 2, 2, 16, 2 * hw), bf16),
             pltpu.VMEM((images, 2, 2, 16, 2 * hw), bf16),
-            pltpu.VMEM((2, 16, 2 * hw), bf16),
+            pltpu.VMEM((2, 2, 16, 2 * hw), bf16),
             pltpu.VMEM((tokens, hw), bf16),
             pltpu.VMEM((tokens, hw), bf16),
             pltpu.VMEM((tokens, hw), bf16),
@@ -543,23 +525,22 @@
 
 
 def scatter_kernel(
-    gkv_ref, kw_hbm, vw_hbm, kws_hbm, vws_hbm, out_ref,
-    weights, mine, theirs, px, py, pz, rx1, rx2, ry1, ry2, zx, zx4, zy, zy4, rz, ty, tz, ly, lz,
-    total, col, col_out, col_in, send_sem, recv_sem, local_sem,
+    gkv_ref, kw_hbm, vw_hbm, theirs_hbm, out_ref,
+    weights, mine, theirs, px, py, pz, rx1, rx2, ry1, ry2, zx, zx4, zy, zy4, rz, rz4, ty, ly, tz, lz,
+    total, col, col_x, col_yz, in_x, in_yz, send_sem, recv_sem, local_sem,
 ):
     x, y, z, c = place()
     links = Links(send_sem, recv_sem)
     right, left = device(turn(x, 1, NX), y, z, c), device(turn(x, -1, NX), y, z, c)
     north, south = device(x, turn(y, 1, NY), z, c), device(x, turn(y, -1, NY), z, c)
-    along = {d: device(x, y, turn(z, d, NZ), c) for d in (-2, -1, 1, 2)}
+    along = {d: device(x, y, turn(z, d, NZ), c) for d in (-1, 1)}
     other = device(x, y, z, 1 - c)
     hw = kw_hbm.shape[1]
     width = kw_hbm.shape[0]
-    rest = width - YCUT
     nt = (((1,), (1,)), ((), ()))
     greet(x, y, z, c)
     loads = [pltpu.make_async_copy(gkv_ref.at[c], mine, local_sem.at[0])]
-    for i, ref in enumerate((kw_hbm, vw_hbm, kws_hbm, vws_hbm)):
+    for i, ref in enumerate((kw_hbm, vw_hbm, theirs_hbm.at[0], theirs_hbm.at[1])):
         loads.append(pltpu.make_async_copy(ref, weights.at[i], local_sem.at[1 + i]))
     for copy in loads:
         copy.start()
@@ -600,11 +581,11 @@
         for i, k in enumerate(ks):
             part = r[i * n : (i + 1) * n]
             px[at[k]] = part[:, :XCUT].reshape(NX, CAP, 16, XCUT)
+            pz[at[k]] = part[:, YCUT:].reshape(NX, CAP, 16, width - YCUT)
             for j in range(NY):
                 py[at[k], j] = part[:, XCUT + j * QUARTER : XCUT + (j + 1) * QUARTER].reshape(
                     NX, CAP, 16, QUARTER
                 )
-            pz[at[k]] = part[:, YCUT:].reshape(NX, CAP, 16, rest)
 
     class First:
         def __init__(self, axis, k):
@@ -647,63 +628,35 @@
             plus(self.part.at[self.own], self.r2[self.i, 0], self.r2[self.i, 1])
 
     def block(axis, k, cut=None):
-        ref = px.at[at[k], x] if axis == 0 else py.at[at[k], y]
+        ref = (px.at[at[k], x], py.at[at[k], y], pz.at[at[k]])[axis]
         return ref if cut is None else ref.at[cut]
 
     def zcuts(axis):
-        return (few, many) if axis == 0 else (pl.ds(0, 3), pl.ds(3, 1))
-
-    def z_far(axis):
-        land, land4 = (zx, zx4) if axis == 0 else (zy, zy4)
-        cuts = zcuts(axis)
-        go = []
-        for s, d in ((0, 1), (1, -1)):
-            near = links.send(block(axis, 3 * d), land.at[0, s], along[d])
-            cut = cuts[1 - s]
-            wide = links.send(
-                block(axis, 4, cut), land4.at[s, pl.ds(0, cut.size)], along[2 * d]
-            )
-            go.append((near, wide))
-        return go
-
-    def z_mid(axis, go):
-        land, land4 = (zx, zx4) if axis == 0 else (zy, zy4)
-        cuts = zcuts(axis)
+        return ((few, many), (pl.ds(0, 3), pl.ds(3, 1)), (front, back))[axis]
+
+    def z_send(axis, k, go):
+        land, land4 = ((zx, zx4), (zy, zy4), (rz, rz4))[axis]
         out = []
         for s, d in ((0, 1), (1, -1)):
-            near, wide = go[s]
-            arrive(near)
-            plus(block(axis, 2 * d), land[0, s])
-            cut = cuts[1 - s]
-            arrive(wide)
-            plus(block(axis, 2 * d, cut), land4[s, pl.ds(0, cut.size)])
-            out.append(links.send(block(axis, 2 * d), land.at[1, s], along[2 * d]))
+            cut = zcuts(axis)[s]
+            if k == 4:
+                out.append(links.send(block(axis, 4, cut), land4.at[s, pl.ds(0, cut.size)], along[d]))
+                continue
+            arrive(go[s])
+            if k == 3:
+                plus(block(axis, 3 * d, cut), land4[s, pl.ds(0, cut.size)])
+            else:
+                plus(block(axis, k * d), land[2 - k, s])
+            out.append(links.send(block(axis, k * d), land.at[3 - k, s], along[d]))
         return out
 
-    def z_near(axis):
-        land = zx if axis == 0 else zy
-        return [
-            links.send(block(axis, d), land.at[2, s], along[d]) for s, d in ((0, 1), (1, -1))
-        ]
-
-    def z_sum(axis):
-        land = zx if axis == 0 else zy
+    def z_sum(axis, go):
+        land = (zx, zy, rz)[axis]
+        arrive(*go)
         value = block(axis, 0)[...].astype(f32)
-        for i in (1, 2):
-            for s in (0, 1):
-                value = value + land[i, s].astype(f32)
+        for s in (0, 1):
+            value = value + land[2, s].astype(f32)
         return value
-
-    def z_ring(step, go):
-        k = 4 - step
-        out = []
-        for s, d in ((0, 1), (1, -1)):
-            cut = (front, back)[s] if step == 1 else pl.ds(0, NX)
-            arrive(go[s])
-            plus(pz.at[at[k * d], cut], rz[s, step - 1, cut])
-            if k:
-                out.append(links.send(pz.at[at[k * d]], rz.at[s, step], along[d]))
-        return out
 
     def over_x(value, mine_ref, land):
         mine_ref[...] = value.astype(bf16)
@@ -717,96 +670,101 @@
 
     def begin(*ks):
         for k in ks:
-            for axis in (0, 1):
+            for axis in (1, 0):
                 first[axis, k] = First(axis, k)
 
     def forward(*ks):
         for k in ks:
-            for axis in (0, 1):
+            for axis in (1, 0):
                 first[axis, k].forward()
 
     def end(*ks):
-        for axis in (0, 1):
+        for axis in (1, 0):
             for k in ks:
                 first[axis, k].end()
 
     project(4)
     begin(4)
-    go_z = [
-        links.send(pz.at[at[4], front], rz.at[0, 0, front], along[1]),
-        links.send(pz.at[at[4], back], rz.at[1, 0, back], along[-1]),
-    ]
+    go_z = z_send(2, 4, None)
     project(3, -3)
     begin(3, -3)
     forward(4)
+    go_z = z_send(2, 3, go_z)
     project(2, -2)
     begin(2, -2)
-    go_z = z_ring(1, go_z)
     forward(3, -3)
     end(4)
+    go_y, go_x = z_send(1, 4, None), z_send(0, 4, None)
+    go_z = z_send(2, 2, go_z)
     project(1, -1)
     begin(1, -1)
-    go_z = z_ring(2, go_z)
     end(3, -3)
-    far_x, far_y = z_far(0), z_far(1)
+    go_y, go_x = z_send(1, 3, go_y), z_send(0, 3, go_x)
+    go_z = z_send(2, 1, go_z)
     forward(2, -2)
     project(0)
     begin(0)
-    go_z = z_ring(3, go_z)
     end(2, -2)
+    go_y, go_x = z_send(1, 2, go_y), z_send(0, 2, go_x)
+    end_z = over_x(z_sum(2, go_z), lz, tz)
     forward(1, -1)
-    mid_y = z_mid(1, far_y)
-    mid_x = z_mid(0, far_x)
-    z_ring(4, go_z)
-    end_z = over_x(pz[z].astype(f32), lz, tz)
     forward(0)
     end(1, -1)
-    near_y, near_x = z_near(1), z_near(0)
+    go_y, go_x = z_send(1, 1, go_y), z_send(0, 1, go_x)
     end(0)
-    arrive(*mid_y, *near_y)
-    end_y = over_x(z_sum(1), ly, ty)
-    arrive(*mid_x, *near_x)
-    total[:, :, :XCUT] = z_sum(0)
-    arrive(*end_z)
-    value = lz[x].astype(f32)
-    for i in range(3):
-        value = value + tz[i].astype(f32)
-    total[:, :, XCUT + QUARTER :] = value
-    arrive(*end_y)
-    value = ly[x].astype(f32)
-    for i in range(3):
-        value = value + ty[i].astype(f32)
-    total[:, :, XCUT : XCUT + QUARTER] = value
-
-    for j in range(NY):
-        for p in range(CAP):
-            col[j, 4 * p : 4 * p + 4, :] = total[p, 4 * j : 4 * j + 4, :]
-        col[j, 12:16, :] = jnp.zeros((4, total.shape[-1]), f32)
-        col_out[j] = col[j].astype(bf16)
-    ends = []
-    for i, d in enumerate((1, 3, 2)):
-        yy = turn(y, d, NY)
-        ends.append(links.send(col_out.at[yy], col_in.at[i], device(x, yy, z, c)))
-    result = col[y]
+    end_y = over_x(z_sum(1, go_y), ly, ty)
+
+    def over_y(cols, cut):
+        for j in range(NY):
+            for p in range(CAP):
+                col[j, 4 * p : 4 * p + 4, cols] = total[p, 4 * j : 4 * j + 4, cols]
+            col[j, 12:16, cols] = jnp.zeros((4, cols.stop - cols.start), f32)
+            (col_x, col_yz)[cut][j] = col[j, :, cols].astype(bf16)
+        out, land = ((col_x, in_x), (col_yz, in_yz))[cut]
+        ends = []
+        for i, d in enumerate((1, 3, 2)):
+            yy = turn(y, d, NY)
+            ends.append(links.send(out.at[yy], land.at[i], device(x, yy, z, c)))
+        return ends
+
+    xs, yzs = slice(0, XCUT), slice(XCUT, total.shape[-1])
+    total[:, :, xs] = z_sum(0, go_x)
+    end_x = over_y(xs, 0)
+    for cols, ends, own, land in (
+        (slice(XCUT + QUARTER, total.shape[-1]), end_z, lz, tz),
+        (slice(XCUT, XCUT + QUARTER), end_y, ly, ty),
+    ):
+        arrive(*ends)
+        value = own[x].astype(f32)
+        for i in range(3):
+            value = value + land[i].astype(f32)
+        total[:, :, cols] = value
+    end_yz = over_y(yzs, 1)
 
     def quarter(j):
         return pl.ds(pl.multiple_of(XCUT + j * QUARTER, 128), QUARTER)
 
+    arrive(*end_x)
+    result = col[y, :, xs]
+    for i in range(3):
+        result = result + in_x[i].astype(f32)
     for p in range(CAP):
-        out_ref[p, :, quarter(y)] = result[4 * p : 4 * p + 4, XCUT : XCUT + QUARTER]
+        out_ref[p, :, :XCUT] = result[4 * p : 4 * p + 4]
+    result = col[y, :, yzs]
+    for p in range(CAP):
+        out_ref[p, :, quarter(y)] = result[4 * p : 4 * p + 4, :QUARTER]
     for i, d in enumerate((1, 3, 2)):
-        arrive(ends[i])
-        got = col_in[i].astype(f32)
+        arrive(end_yz[i])
+        got = in_yz[i].astype(f32)
         for p in range(CAP):
-            out_ref[p, :, quarter(turn(y, -d, NY))] = got[4 * p : 4 * p + 4, XCUT : XCUT + QUARTER]
+            out_ref[p, :, quarter(turn(y, -d, NY))] = got[4 * p : 4 * p + 4, :QUARTER]
         result = result + got
     for p in range(CAP):
-        out_ref[p, :, :XCUT] = result[4 * p : 4 * p + 4, :XCUT]
-        out_ref[p, :, YCUT:] = result[4 * p : 4 * p + 4, XCUT + QUARTER :]
+        out_ref[p, :, YCUT:] = result[4 * p : 4 * p + 4, QUARTER:]
     links.finish()
 
 
-def scatter_latents(gkv, kw, vw, kws, vws):
+def scatter_latents(gkv, kw, vw, theirs):
     width, hw = kw.shape
     rest = width - YCUT
     last = XCUT + QUARTER + rest
@@ -819,7 +777,7 @@
         scatter_kernel,
         name="scatter_latents",
         out_shape=jax.ShapeDtypeStruct((CAP, 4, width), f32),
-        in_specs=[hbm, hbm, hbm, hbm, hbm],
+        in_specs=[hbm, hbm, hbm, hbm],
         out_specs=pl.BlockSpec(memory_space=pltpu.VMEM),
         scratch_shapes=[
             buffer(4, width, hw),
@@ -836,34 +794,37 @@
             buffer(2, 2, 16, XCUT),
             buffer(3, 2, NX, CAP, 16, QUARTER),
             buffer(2, 3, CAP, 16, QUARTER),
-            buffer(2, 4, NX, CAP, 16, rest),
+            buffer(3, 2, NX, CAP, 16, rest),
+            buffer(2, 2, CAP, 16, rest),
             buffer(3, CAP, 16, QUARTER),
+            buffer(NX, CAP, 16, QUARTER),
             buffer(3, CAP, 16, rest),
-            buffer(NX, CAP, 16, QUARTER),
             buffer(NX, CAP, 16, rest),
             pltpu.VMEM((CAP, 16, last), f32),
             pltpu.VMEM((NY, 16, last), f32),
-            buffer(NY, 16, last),
-            buffer(3, 16, last),
+            buffer(NY, 16, XCUT),
+            buffer(NY, 16, QUARTER + rest),
+            buffer(3, 16, XCUT),
+            buffer(3, 16, QUARTER + rest),
             pltpu.SemaphoreType.DMA((SCATTER_SEMS,)),
             pltpu.SemaphoreType.DMA((SCATTER_SEMS,)),
             pltpu.SemaphoreType.DMA((5,)),
         ],
         compiler_params=pltpu.CompilerParams(
-            collective_id=1, has_side_effects=True, vmem_limit_bytes=62 << 20
+            collective_id=1, has_side_effects=True, vmem_limit_bytes=52 << 20
         ),
-    )(gkv, kw, vw, kws, vws)
+    )(gkv, kw, vw, theirs)
 
 
 def on_device(
     latents, key_weight, value_weight, gate_logit, queries, cotangent, image_counts, token_image
 ):
     kw, vw = key_weight[0], value_weight[0]
-    kv, kws, vws = gather_latents(latents, kw, vw)
+    kv, theirs = gather_latents(latents, kw, vw)
     attended, grad_queries, gkv = attention(
         image_counts, gate_logit, token_image, kv, queries[0], cotangent[0]
     )
-    grad_latents = scatter_latents(gkv, kw, vw, kws, vws)
+    grad_latents = scatter_latents(gkv, kw, vw, theirs)
     return attended[None], grad_queries[None], grad_latents
 
 

time: 96.6 us -> 94.5 us (0.978)
  Pallas kernels: 93.6 us -> 92.2 us
    pallas_call x1, Pallas kernels: 42.3 us -> 40.8 us  [scatter_latents(): pl.pallas_call(scatter_kernel, name='scatter_latents', out_shape=jax.Shap...]
where the time goes in v3:
time: 94.5 us; the launch traced here: 94.3 us
  Pallas kernels  92.2 us (98%)
  between operations  1.43 us (2%)
    pallas_call x1, Pallas kernels, gather_latents(): pl.pallas_call(gather_kernel, name='gather_latents', out_shape=(jax.Shape...  42.1 us
    pallas_call x1, Pallas kernels, scatter_latents(): pl.pallas_call(scatter_kernel, name='scatter_latents', out_shape=jax.Shap...  40.8 us
    pallas_call x1, Pallas kernels, attention(): pl.pallas_call(attention_kernel, name='attention', out_shape=(jax.ShapeDt...  9.31 us

profile of v3, /device:TPU:8, one launch (start us, length us, event | category | flops | bytes accessed | tf_op | source)
XLA Modules:
  0.0 94.3 jit_solution(1123662718649910335)
XLA Ops:
  0.6 0.0 copy-start.1
  0.6 0.0 copy-start
  1.4 42.1 %gather_latents.1 = (bf16[2,8,4,3,16,512]{5,4,3,2,1,0:T(8,128)(2,1)}, bf16[2,1280,256]{2,1,0:T(8,128)(2,1)}) custom-call(bf16[3,4,1280]{2,1,0:T(4,128)(2,1)} %own_hbm.1, bf16[1280,256]{1,0:T(8,128)(2,1)} %bitcast.7, bf16[1280,256]{1,0:T(8,128)(2,1)} %bitcast.9), custom_call_target="tpu_custom_call" | custom-call | tf_op jit(solution)/shard_map/gather_latents/pallas_call | solution.py:286
  43.5 9.3 %attention.1 = (bf16[1024,256]{1,0:T(8,128)(2,1)}, bf16[1024,256]{1,0:T(8,128)(2,1)}, bf16[2,8,4,3,16,512]{5,4,3,2,1,0:T(8,128)(2,1)}) custom-call(s32[16]{0:T(128)} %counts_ref.1, f32[1]{0:T(128)S(6)} %copy.12.gate_ref, s32[8,128]{1,0:T(8,128)} %bitcast.13, bf16[2,8,4,3,16,512]{5,4,3,2,1,0:T(8,128)(2,1)} %get-tuple-element.8.kv_ref, ...), custom_call_target="tpu_custom_call" | custom-call | tf_op jit(solution)/shard_map/attention/pallas_call | solution.py:493
  52.8 0.0 copy-done.1
  52.8 0.0 copy-done
  52.8 40.8 %scatter_latents.1 = f32[3,4,1280]{2,1,0:T(4,128)S(1)} custom-call(bf16[2,8,4,3,16,512]{5,4,3,2,1,0:T(8,128)(2,1)} %get-tuple-element.11.gkv_ref, bf16[1280,256]{1,0:T(8,128)(2,1)S(1)} %bitcast.8, bf16[1280,256]{1,0:T(8,128)(2,1)S(1)} %bitcast.10, bf16[2,1280,256]{2,1,0:T(8,128)(2,1)} %get-tuple-element.12.theirs_hbm), custom_call_target="tpu_custom_call" | custom-call | tf_op jit(solution)/shard_map/scatter_latents/pallas_call | solution.py:776
  93.6 0.6 copy.13
Async XLA Ops:
  0.6 52.2 %copy-start.1 = (bf16[1,1280,256]{2,1,0:T(8,128)(2,1)S(1)}, bf16[1,1280,256]{2,1,0:T(8,128)(2,1)}, u32[]{:S(2)}) copy-start(bf16[1,1280,256]{2,1,0:T(8,128)(2,1)} %param.10) | copy-start | bytes 1966084
  0.6 52.2 %copy-start = (bf16[1,1280,256]{2,1,0:T(8,128)(2,1)S(1)}, bf16[1,1280,256]{2,1,0:T(8,128)(2,1)}, u32[]{:S(2)}) copy-start(bf16[1,1280,256]{2,1,0:T(8,128)(2,1)} %param.9) | copy-start | bytes 1966084

commit v4 on v3

--- a/solution.py
+++ b/solution.py
@@ -58,9 +58,11 @@
             copy.wait_send()
 
 
+STEPS = [(dx, dy) for dx in range(NX) for dy in range(NY) if dx or dy]
+
+
 def greet(x, y, z, c):
-    peers = [device(x, turn(y, d, NY), z, c) for d in (1, 2, 3)]
-    peers += [device(turn(x, d, NX), y, z, c) for d in (1, 2, 3)]
+    peers = [device(turn(x, dx, NX), turn(y, dy, NY), z, c) for dx, dy in STEPS]
     peers += [device(x, y, turn(z, d, NZ), c) for d in (1, -1)]
     peers += [device(x, y, z, 1 - c)]
     barrier = pltpu.get_barrier_semaphore()
@@ -69,7 +71,7 @@
 
 
 def meet():
-    pl.semaphore_wait(pltpu.get_barrier_semaphore(), NX + NY + 1)
+    pl.semaphore_wait(pltpu.get_barrier_semaphore(), len(STEPS) + 3)
 
 
 GATHER_SEMS = 160
@@ -78,7 +80,7 @@
 
 def gather_kernel(
     own_hbm, kw_ref, vw_ref, kv_ref, theirs_ref,
-    hx, hy, hz, own, mine, column, rows, weights, kv, kv_out, send_sem, recv_sem, local_sem,
+    hx, hy, hz, own, mine, column, rows, out_yz, in_yz, rows_yz, weights, kv, kv_out, send_sem, recv_sem, local_sem,
 ):
     x, y, z, c = place()
     links = Links(send_sem, recv_sem)
@@ -101,23 +103,27 @@
     for p in range(CAP):
         mine[4 * p : 4 * p + 4, :] = own[p].astype(f32)
     mine[12:16, :] = jnp.zeros((4, width), f32)
-    column[y] = mine[...].astype(bf16)
+    column[y] = mine[:, :XCUT].astype(bf16)
+    for j in range(NY):
+        out_yz[j, 0] = mine[:, XCUT + j * QUARTER : XCUT + (j + 1) * QUARTER].astype(bf16)
+        out_yz[j, 1] = mine[:, YCUT:].astype(bf16)
     meet()
 
     firsts = []
     for d in (1, 3, 2):
         firsts.append(links.send(column.at[y], column.at[y], device(x, turn(y, d, NY), z, c)))
-
+    seconds = []
+    for dx, dy in STEPS:
+        xx, yy = turn(x, dx, NX), turn(y, dy, NY)
+        seconds.append(links.send(out_yz.at[yy], in_yz.at[x, y], device(xx, yy, z, c)))
+    in_yz[x, y] = out_yz[y]
     for copy in firsts:
         copy.wait_recv()
     for j in range(NY):
-        block = column[j].astype(f32)
+        piece = column[j].astype(f32)
         for p in range(CAP):
-            rows[p, 4 * j : 4 * j + 4, :] = block[4 * p : 4 * p + 4, :]
-    part = pl.ds(pl.multiple_of(XCUT + y * QUARTER, 128), QUARTER)
-    hx[z, x] = rows[:, :, :XCUT].astype(bf16)
-    hy[z, y, x] = rows[:, :, part].astype(bf16)
-    hz[z, x] = rows[:, :, YCUT:].astype(bf16)
+            rows[p, 4 * j : 4 * j + 4, :] = piece[4 * p : 4 * p + 4, :]
+    hx[z, x] = rows[...].astype(bf16)
 
     def send(ref, dev):
         return links.send(ref, ref, dev)
@@ -127,11 +133,11 @@
             copy.wait_recv()
 
     stores = []
-    swaps = {}
-
-    def store(i, zz):
+    swaps = []
+
+    def store(zz):
         j = 3 + len(stores)
-        copy = pltpu.make_async_copy(kv.at[i, zz], kv_ref.at[i, zz], local_sem.at[j])
+        copy = pltpu.make_async_copy(kv.at[zz], kv_ref.at[c, zz], local_sem.at[j])
         copy.start()
         stores.append(copy)
 
@@ -146,21 +152,15 @@
             r = r.reshape(NX, CAP, 16, hw)
             cols = slice((i % 2) * hw, (i % 2 + 1) * hw)
             if i < 2:
-                kv[c, zz, :, :, :, cols] = r
+                kv[zz, :, :, :, cols] = r
             else:
                 kv_out[zz, :, :, :, cols] = r
             if i == 3:
-                swaps[len(swaps)] = zz, links.send(kv_out.at[zz], kv.at[c, zz], other)
-        store(c, zz)
-
-    def swapped(i):
-        zz, copy = swaps[i]
-        copy.wait_recv()
-        store(1 - c, zz)
+                swaps.append(links.send(kv_out.at[zz], kv_ref.at[c, zz], other))
+        store(zz)
 
     x1, x3 = turn(x, 1, NX), turn(x, -1, NX)
     y1, y3 = turn(y, 1, NY), turn(y, -1, NY)
-    xpeers = [device(turn(x, d, NX), y, z, c) for d in (1, 3, 2)]
     few, many = pl.ds(0, 1), pl.ds(1, 2)
     front, back = pl.ds(0, 2), pl.ds(2, 2)
 
@@ -212,15 +212,20 @@
 
     for copy in loads:
         copy.wait()
-    y_first = [send(hy.at[z, y, x], dev) for dev in xpeers]
-    z_first = [send(hz.at[z, x], dev) for dev in xpeers]
     go_x = over_z(0)
     swap_w = [links.send(weights.at[i], weights.at[2 + i], other) for i in (0, 1)]
     last = {(0, 0): Last(0, 0)}
-    arrive(*y_first)
+    arrive(*seconds)
+    for i in range(NX):
+        for j in range(NY):
+            piece = in_yz[i, j].astype(f32)
+            for p in range(CAP):
+                for s in range(2):
+                    rows_yz[s, p, 4 * j : 4 * j + 4, :] = piece[s, 4 * p : 4 * p + 4, :]
+        hy[z, y, i] = rows_yz[0].astype(bf16)
+        hz[z, i] = rows_yz[1].astype(bf16)
     go_y = over_z(1)
     last[1, 0] = Last(1, 0)
-    arrive(*z_first)
     go_z = over_z(2)
 
     def finish(k):
@@ -271,8 +276,7 @@
     end(4)
     finish(4)
 
-    for i in range(NZ):
-        swapped(i)
+    arrive(*swaps)
     theirs.wait()
     for copy in stores:
         copy.wait()
@@ -298,14 +302,17 @@
             pltpu.VMEM((NZ, NX, CAP, 16, width - YCUT), bf16),
             pltpu.VMEM(latents.shape, bf16),
             pltpu.VMEM((16, width), f32),
-            pltpu.VMEM((NY, 16, width), bf16),
-            pltpu.VMEM((CAP, 16, width), f32),
+            pltpu.VMEM((NY, 16, XCUT), bf16),
+            pltpu.VMEM((CAP, 16, XCUT), f32),
+            pltpu.VMEM((NY, 2, 16, QUARTER), bf16),
+            pltpu.VMEM((NX, NY, 2, 16, QUARTER), bf16),
+            pltpu.VMEM((2, CAP, 16, QUARTER), f32),
             pltpu.VMEM((4,) + key_weight.shape, bf16),
-            pltpu.VMEM((2, NZ, NX, CAP, 16, 2 * hw), bf16),
+            pltpu.VMEM((NZ, NX, CAP, 16, 2 * hw), bf16),
             pltpu.VMEM((NZ, NX, CAP, 16, 2 * hw), bf16),
             pltpu.SemaphoreType.DMA((GATHER_SEMS,)),
             pltpu.SemaphoreType.DMA((GATHER_SEMS,)),
-            pltpu.SemaphoreType.DMA((3 + 2 * NZ,)),
+            pltpu.SemaphoreType.DMA((3 + NZ,)),
         ],
         compiler_params=pltpu.CompilerParams(
             collective_id=0, has_side_effects=True, vmem_limit_bytes=62 << 20
@@ -526,8 +533,8 @@
 
 def scatter_kernel(
     gkv_ref, kw_hbm, vw_hbm, theirs_hbm, out_ref,
-    weights, mine, theirs, px, py, pz, rx1, rx2, ry1, ry2, zx, zx4, zy, zy4, rz, rz4, ty, ly, tz, lz,
-    total, col, col_x, col_yz, in_x, in_yz, send_sem, recv_sem, local_sem,
+    weights, mine, theirs, px, py, pz, rx1, rx2, ry1, ry2, zx, zx4, zy, zy4, rz, rz4, tz, lz,
+    total, col, col_out, col_in, col_y, out_y, in_y, send_sem, recv_sem, local_sem,
 ):
     x, y, z, c = place()
     links = Links(send_sem, recv_sem)
@@ -712,62 +719,56 @@
     end(1, -1)
     go_y, go_x = z_send(1, 1, go_y), z_send(0, 1, go_x)
     end(0)
-    end_y = over_x(z_sum(1, go_y), ly, ty)
-
-    def over_y(cols, cut):
+    value = z_sum(1, go_y)
+    for i in range(NX):
         for j in range(NY):
             for p in range(CAP):
-                col[j, 4 * p : 4 * p + 4, cols] = total[p, 4 * j : 4 * j + 4, cols]
-            col[j, 12:16, cols] = jnp.zeros((4, cols.stop - cols.start), f32)
-            (col_x, col_yz)[cut][j] = col[j, :, cols].astype(bf16)
-        out, land = ((col_x, in_x), (col_yz, in_yz))[cut]
-        ends = []
-        for i, d in enumerate((1, 3, 2)):
-            yy = turn(y, d, NY)
-            ends.append(links.send(out.at[yy], land.at[i], device(x, yy, z, c)))
-        return ends
-
-    xs, yzs = slice(0, XCUT), slice(XCUT, total.shape[-1])
-    total[:, :, xs] = z_sum(0, go_x)
-    end_x = over_y(xs, 0)
-    for cols, ends, own, land in (
-        (slice(XCUT + QUARTER, total.shape[-1]), end_z, lz, tz),
-        (slice(XCUT, XCUT + QUARTER), end_y, ly, ty),
-    ):
-        arrive(*ends)
-        value = own[x].astype(f32)
-        for i in range(3):
-            value = value + land[i].astype(f32)
-        total[:, :, cols] = value
-    end_yz = over_y(yzs, 1)
-
-    def quarter(j):
-        return pl.ds(pl.multiple_of(XCUT + j * QUARTER, 128), QUARTER)
-
-    arrive(*end_x)
-    result = col[y, :, xs]
+                col_y[i, j, 4 * p : 4 * p + 4, :] = value[i, p, 4 * j : 4 * j + 4, :]
+            col_y[i, j, 12:16, :] = jnp.zeros((4, QUARTER), f32)
+            out_y[i, j] = col_y[i, j].astype(bf16)
+    end_y = []
+    for i, (dx, dy) in enumerate(STEPS):
+        xx, yy = turn(x, dx, NX), turn(y, dy, NY)
+        end_y.append(links.send(out_y.at[xx, yy], in_y.at[i], device(xx, yy, z, c)))
+
+    total[:, :, :XCUT] = z_sum(0, go_x)
+    arrive(*end_z)
+    value = lz[x].astype(f32)
     for i in range(3):
-        result = result + in_x[i].astype(f32)
+        value = value + tz[i].astype(f32)
+    total[:, :, XCUT:] = value
+    for j in range(NY):
+        for p in range(CAP):
+            col[j, 4 * p : 4 * p + 4, :] = total[p, 4 * j : 4 * j + 4, :]
+        col[j, 12:16, :] = jnp.zeros((4, total.shape[-1]), f32)
+        col_out[j] = col[j].astype(bf16)
+    ends = []
+    for i, d in enumerate((1, 3, 2)):
+        yy = turn(y, d, NY)
+        ends.append(links.send(col_out.at[yy], col_in.at[i], device(x, yy, z, c)))
+    arrive(*end_y)
+    for d in range(NY):
+        cols = pl.ds(pl.multiple_of(XCUT + turn(y, -d, NY) * QUARTER, 128), QUARTER)
+        terms = [in_y[i].astype(f32) for i, (dx, dy) in enumerate(STEPS) if dy == d]
+        if d == 0:
+            terms.append(col_y[x, y])
+        value = sum(terms[1:], terms[0])
+        for p in range(CAP):
+            out_ref[p, :, cols] = value[4 * p : 4 * p + 4]
+    arrive(*ends)
+    result = col[y]
+    for i in range(3):
+        result = result + col_in[i].astype(f32)
     for p in range(CAP):
-        out_ref[p, :, :XCUT] = result[4 * p : 4 * p + 4]
-    result = col[y, :, yzs]
-    for p in range(CAP):
-        out_ref[p, :, quarter(y)] = result[4 * p : 4 * p + 4, :QUARTER]
-    for i, d in enumerate((1, 3, 2)):
-        arrive(end_yz[i])
-        got = in_yz[i].astype(f32)
-        for p in range(CAP):
-            out_ref[p, :, quarter(turn(y, -d, NY))] = got[4 * p : 4 * p + 4, :QUARTER]
-        result = result + got
-    for p in range(CAP):
-        out_ref[p, :, YCUT:] = result[4 * p : 4 * p + 4, QUARTER:]
+        out_ref[p, :, :XCUT] = result[4 * p : 4 * p + 4, :XCUT]
+        out_ref[p, :, YCUT:] = result[4 * p : 4 * p + 4, XCUT:]
     links.finish()
 
 
 def scatter_latents(gkv, kw, vw, theirs):
     width, hw = kw.shape
     rest = width - YCUT
-    last = XCUT + QUARTER + rest
+    last = XCUT + rest
     hbm = pl.BlockSpec(memory_space=pltpu.HBM)
 
     def buffer(*shape):
@@ -796,16 +797,15 @@
             buffer(2, 3, CAP, 16, QUARTER),
             buffer(3, 2, NX, CAP, 16, rest),
             buffer(2, 2, CAP, 16, rest),
-            buffer(3, CAP, 16, QUARTER),
-            buffer(NX, CAP, 16, QUARTER),
             buffer(3, CAP, 16, rest),
             buffer(NX, CAP, 16, rest),
             pltpu.VMEM((CAP, 16, last), f32),
             pltpu.VMEM((NY, 16, last), f32),
-            buffer(NY, 16, XCUT),
-            buffer(NY, 16, QUARTER + rest),
-            buffer(3, 16, XCUT),
-            buffer(3, 16, QUARTER + rest),
+            buffer(NY, 16, last),
+            buffer(3, 16, last),
+            pltpu.VMEM((NX, NY, 16, QUARTER), f32),
+            buffer(NX, NY, 16, QUARTER),
+            buffer(len(STEPS), 16, QUARTER),
             pltpu.SemaphoreType.DMA((SCATTER_SEMS,)),
             pltpu.SemaphoreType.DMA((SCATTER_SEMS,)),
             pltpu.SemaphoreType.DMA((5,)),

time: 94.5 us -> 91.8 us (0.971)
  Pallas kernels: 92.2 us -> 89.2 us
    pallas_call x1, Pallas kernels: 40.8 us -> 39.2 us  [scatter_latents(): pl.pallas_call(scatter_kernel, name='scatter_latents', out_shape=jax.Shap...]
    pallas_call x1, Pallas kernels: 42.1 us -> 40.7 us  [gather_latents(): pl.pallas_call(gather_kernel, name='gather_latents', out_shape=(jax.Shape...]
where the time goes in v4:
time: 91.8 us; the launch traced here: 91.3 us
  Pallas kernels  89.2 us (97%)
  between operations  1.43 us (2%)
    pallas_call x1, Pallas kernels, gather_latents(): pl.pallas_call(gather_kernel, name='gather_latents', out_shape=(jax.Shape...  40.7 us
    pallas_call x1, Pallas kernels, scatter_latents(): pl.pallas_call(scatter_kernel, name='scatter_latents', out_shape=jax.Shap...  39.2 us
    pallas_call x1, Pallas kernels, attention(): pl.pallas_call(attention_kernel, name='attention', out_shape=(jax.ShapeDt...  9.31 us

profile of v4, /device:TPU:8, one launch (start us, length us, event | category | flops | bytes accessed | tf_op | source)
XLA Modules:
  0.0 91.3 jit_solution(4263823769906032376)
XLA Ops:
  0.6 0.0 copy-start.1
  0.6 0.0 copy-start
  1.4 40.7 %gather_latents.1 = (bf16[2,8,4,3,16,512]{5,4,3,2,1,0:T(8,128)(2,1)}, bf16[2,1280,256]{2,1,0:T(8,128)(2,1)}) custom-call(bf16[3,4,1280]{2,1,0:T(4,128)(2,1)} %own_hbm.1, bf16[1280,256]{1,0:T(8,128)(2,1)} %bitcast.7, bf16[1280,256]{1,0:T(8,128)(2,1)} %bitcast.9), custom_call_target="tpu_custom_call" | custom-call | tf_op jit(solution)/shard_map/gather_latents/pallas_call | solution.py:290
  42.1 9.3 %attention.1 = (bf16[1024,256]{1,0:T(8,128)(2,1)}, bf16[1024,256]{1,0:T(8,128)(2,1)}, bf16[2,8,4,3,16,512]{5,4,3,2,1,0:T(8,128)(2,1)}) custom-call(s32[16]{0:T(128)} %counts_ref.1, f32[1]{0:T(128)S(6)} %copy.12.gate_ref, s32[8,128]{1,0:T(8,128)} %bitcast.13, bf16[2,8,4,3,16,512]{5,4,3,2,1,0:T(8,128)(2,1)} %get-tuple-element.8.kv_ref, ...), custom_call_target="tpu_custom_call" | custom-call | tf_op jit(solution)/shard_map/attention/pallas_call | solution.py:500
  51.5 0.0 copy-done.1
  51.5 0.0 copy-done
  51.5 39.2 %scatter_latents.1 = f32[3,4,1280]{2,1,0:T(4,128)S(1)} custom-call(bf16[2,8,4,3,16,512]{5,4,3,2,1,0:T(8,128)(2,1)} %get-tuple-element.11.gkv_ref, bf16[1280,256]{1,0:T(8,128)(2,1)S(1)} %bitcast.8, bf16[1280,256]{1,0:T(8,128)(2,1)S(1)} %bitcast.10, bf16[2,1280,256]{2,1,0:T(8,128)(2,1)} %get-tuple-element.12.theirs_hbm), custom_call_target="tpu_custom_call" | custom-call | tf_op jit(solution)/shard_map/scatter_latents/pallas_call | solution.py:777
  90.7 0.6 copy.13
Async XLA Ops:
  0.6 50.8 %copy-start.1 = (bf16[1,1280,256]{2,1,0:T(8,128)(2,1)S(1)}, bf16[1,1280,256]{2,1,0:T(8,128)(2,1)}, u32[]{:S(2)}) copy-start(bf16[1,1280,256]{2,1,0:T(8,128)(2,1)} %param.10) | copy-start | bytes 1966084
  0.6 50.8 %copy-start = (bf16[1,1280,256]{2,1,0:T(8,128)(2,1)S(1)}, bf16[1,1280,256]{2,1,0:T(8,128)(2,1)}, u32[]{:S(2)}) copy-start(bf16[1,1280,256]{2,1,0:T(8,128)(2,1)} %param.9) | copy-start | bytes 1966084

commit v5 on v4

--- a/solution.py
+++ b/solution.py
@@ -322,7 +322,7 @@
 
 BLOCK = 128
 CHUNK = 4
-SIDE = 4
+SIDE = 5
 
 
 def attention_kernel(

time: 91.8 us -> 91.4 us (level)
  no operation moved by 1% of the time
where the time goes in v5:
time: 91.4 us; the launch traced here: 90.8 us
  Pallas kernels  88.8 us (97%)
  between operations  1.43 us (2%)
    pallas_call x1, Pallas kernels, gather_latents(): pl.pallas_call(gather_kernel, name='gather_latents', out_shape=(jax.Shape...  40.7 us
    pallas_call x1, Pallas kernels, scatter_latents(): pl.pallas_call(scatter_kernel, name='scatter_latents', out_shape=jax.Shap...  39.1 us
    pallas_call x1, Pallas kernels, attention(): pl.pallas_call(attention_kernel, name='attention', out_shape=(jax.ShapeDt...  8.88 us

profile of v5, /device:TPU:8, one launch (start us, length us, event | category | flops | bytes accessed | tf_op | source)
XLA Modules:
  0.0 90.8 jit_solution(8176525029344540288)
XLA Ops:
  0.6 0.0 copy-start.1
  0.6 0.0 copy-start
  1.4 40.7 %gather_latents.1 = (bf16[2,8,4,3,16,512]{5,4,3,2,1,0:T(8,128)(2,1)}, bf16[2,1280,256]{2,1,0:T(8,128)(2,1)}) custom-call(bf16[3,4,1280]{2,1,0:T(4,128)(2,1)} %own_hbm.1, bf16[1280,256]{1,0:T(8,128)(2,1)} %bitcast.7, bf16[1280,256]{1,0:T(8,128)(2,1)} %bitcast.9), custom_call_target="tpu_custom_call" | custom-call | tf_op jit(solution)/shard_map/gather_latents/pallas_call | solution.py:290
  42.1 8.9 %attention.1 = (bf16[1024,256]{1,0:T(8,128)(2,1)}, bf16[1024,256]{1,0:T(8,128)(2,1)}, bf16[2,8,4,3,16,512]{5,4,3,2,1,0:T(8,128)(2,1)}) custom-call(s32[16]{0:T(128)} %counts_ref.1, f32[1]{0:T(128)S(6)} %copy.12.gate_ref, s32[8,128]{1,0:T(8,128)} %bitcast.13, bf16[2,8,4,3,16,512]{5,4,3,2,1,0:T(8,128)(2,1)} %get-tuple-element.8.kv_ref, ...), custom_call_target="tpu_custom_call" | custom-call | tf_op jit(solution)/shard_map/attention/pallas_call | solution.py:500
  51.0 0.0 copy-done.1
  51.0 0.0 copy-done
  51.1 39.1 %scatter_latents.1 = f32[3,4,1280]{2,1,0:T(4,128)S(1)} custom-call(bf16[2,8,4,3,16,512]{5,4,3,2,1,0:T(8,128)(2,1)} %get-tuple-element.11.gkv_ref, bf16[1280,256]{1,0:T(8,128)(2,1)S(1)} %bitcast.8, bf16[1280,256]{1,0:T(8,128)(2,1)S(1)} %bitcast.10, bf16[2,1280,256]{2,1,0:T(8,128)(2,1)} %get-tuple-element.12.theirs_hbm), custom_call_target="tpu_custom_call" | custom-call | tf_op jit(solution)/shard_map/scatter_latents/pallas_call | solution.py:777
  90.2 0.6 copy.13
Async XLA Ops:
  0.6 50.4 %copy-start.1 = (bf16[1,1280,256]{2,1,0:T(8,128)(2,1)S(1)}, bf16[1,1280,256]{2,1,0:T(8,128)(2,1)}, u32[]{:S(2)}) copy-start(bf16[1,1280,256]{2,1,0:T(8,128)(2,1)} %param.10) | copy-start | bytes 1966084
  0.6 50.4 %copy-start = (bf16[1,1280,256]{2,1,0:T(8,128)(2,1)S(1)}, bf16[1,1280,256]{2,1,0:T(8,128)(2,1)}, u32[]{:S(2)}) copy-start(bf16[1,1280,256]{2,1,0:T(8,128)(2,1)} %param.9) | copy-start | bytes 1966084
